TPU v7x, 32 devices: a whole 2x2x4 slice. The times are simulated.
32 devices in a mesh: row: 4 (over y, core), col: 8 (over z, x).
Axes of the slice: x: 2, y: 2, z: 4, core: 2. Of those that a mesh axis runs over, the one named last changes fastest.
Arguments:
- features: bfloat16 [32768, 128], P('col', 'row'), may hold values from -6 to 6
- block_codes: int32 [4, 3072], P('row', 'col'), may hold values from 0 to 8191
- block_count: int32 [4, 8], P('row', 'col'), may hold values from 1 to 384, as said below
- block_values: bfloat16 [4, 3072, 4096], P('row', 'col'), may hold values from -0.119628906 to 0.119628906
- weight: bfloat16 [128, 256], replicated, may hold values from -0.5 to 0.5
- bias: float32 [256], replicated, may hold values from -3 to 3
Outputs:
- activated: bfloat16 [32768, 256], P(('row', 'col'))
Inputs may be any that keep to these rules, and one draw needn't show every extreme that they name: `block_count`: every tile's count is at most 384; some tile holds exactly 384 in every draw; counts are skewed, the busiest tile about three times the mean. `block_codes`: A code c names local row block c // 64 and local column block c % 64.
All inputs are finite; a program needn't handle non-finite values.
Results may differ from a plain program's by a relative error of at most 0.0045.
Values may be sent and summed in bfloat16 or wider, within the bound.
No kernel may reach another device: no remote copies, remote signals or barrier semaphores. Data moves between devices by JAX's collectives and lax.ppermute only.
A program may use at most 128 MiB of HBM per device.

v0:
```python
import functools

import jax
import jax.numpy as jnp
from jax import lax
from jax.experimental import pallas as pl
from jax.experimental.pallas import tpu as pltpu
from jax.sharding import PartitionSpec as P

BLK = 64
PAIR = BLK // 2
LANES = 2 * BLK
GROUP = 16
TOGETHER = 4
UNROLL = 16
SLOT_AT, SOURCE_AT = 13, 7
MIB = 1024 * 1024
SMEM = pl.BlockSpec(memory_space=pltpu.SMEM)
VMEM = pl.BlockSpec(memory_space=pltpu.VMEM)


def log2(size):
    return size.bit_length() - 1


def list_width(slots):
    return -(-(slots + 2 * UNROLL + 8) // LANES) * LANES


def make_lists(chunks, col_bits, count, codes, words_ref):
    slots, width = codes.shape[1], words_ref.shape[1]
    per = sum(size for size, _ in chunks)
    row_block, col_block = codes >> col_bits, codes & ((1 << col_bits) - 1)
    owner = (row_block >> log2(per)) ^ lax.axis_index("col")
    sub = row_block & (per - 1)
    number = lax.broadcasted_iota(jnp.int32, (1, slots), 1)
    live = number < count
    group, target = jnp.full_like(codes, len(chunks) + 1), jnp.zeros_like(codes)
    first, base = 0, 0
    for c, (size, order) in enumerate(chunks):
        place = jnp.zeros_like(owner)
        for k, bit in enumerate(order):
            place = place | (((owner >> bit) & 1) << (len(order) - 1 - k))
        place = (place << log2(size)) + (sub - first)
        half = size << (len(order) - 1)
        keep = place < half
        here = live & (sub >= first) & (sub < first + size)
        target = jnp.where(here, jnp.where(keep, place + base, place - half), target)
        group = jnp.where(here, jnp.where(keep, len(chunks), c), group)
        first, base = first + size, base + half
    same = lax.broadcasted_iota(jnp.int32, (slots, slots), 0) == lax.broadcasted_iota(jnp.int32, (slots, slots), 1)
    column = lambda row: jnp.sum(jnp.where(same, row, 0.0), axis=1, keepdims=True)
    spot = lax.broadcasted_iota(jnp.int32, (slots, width), 1).astype(jnp.float32)
    lane = lax.broadcasted_iota(jnp.int32, (1, width), 1)
    key = (group * slots + number).astype(jnp.float32)
    word = ((number << SLOT_AT) | (col_block << SOURCE_AT) | target).astype(jnp.float32)
    rank = jnp.sum(jnp.where(key < column(key), 1.0, 0.0), axis=1, keepdims=True)
    words = jnp.sum(jnp.where(rank == spot, column(word), 0.0), axis=0, keepdims=True).astype(jnp.int32)
    for k in range(len(chunks) + 2):
        before = jnp.sum(jnp.where(group < k, 1.0, 0.0), axis=1, keepdims=True).astype(jnp.int32)
        words = jnp.where(lane == width - 8 + k, before, words)
    words_ref[...] = words


def relayout_kernel(chunks, col_bits, count_ref, codes_hbm, values_hbm, out_ref, words_ref, codes, held, scratch, arrived, codes_arrived):
    codes_copy = pltpu.make_async_copy(codes_hbm, codes, codes_arrived)
    codes_copy.start()
    step = GROUP * TOGETHER

    def copy(k):
        rows = pl.ds(pl.multiple_of(k * step, step), step)
        return pltpu.make_async_copy(values_hbm.at[rows], held.at[rows], arrived.at[k])

    steps = values_hbm.shape[0] // step
    for k in range(steps):
        copy(k).start()
    codes_copy.wait()
    make_lists(chunks, col_bits, count_ref[0, 0], codes[...], words_ref)

    def one(k, carry):
        copy(k).wait()
        for g in range(TOGETHER):
            slots = pl.ds(pl.multiple_of(k * step + g * GROUP, GROUP), GROUP)
            for p in range(PAIR):
                wide = held[slots, p * LANES : (p + 1) * LANES].astype(jnp.float32)
                scratch[(g * PAIR + p) * GROUP : (g * PAIR + p + 1) * GROUP, :] = wide
        for g in range(TOGETHER):
            for s in range(GROUP):
                rows = scratch[pl.ds(g * PAIR * GROUP + s, PAIR, stride=GROUP), :]
                at = pl.multiple_of((k * step + g * GROUP + s) * PAIR, PAIR)
                out_ref[pl.ds(at, PAIR), :] = rows.astype(out_ref.dtype)
        return carry

    lax.fori_loop(0, steps, one, 0)


def relayout(chunks, col_bits, count, codes, values):
    slots = values.shape[0]
    return pl.pallas_call(
        functools.partial(relayout_kernel, chunks, col_bits),
        in_specs=[SMEM] + [pl.BlockSpec(memory_space=pltpu.HBM)] * 2,
        out_specs=(VMEM, VMEM),
        out_shape=(
            jax.ShapeDtypeStruct((slots * PAIR, LANES), values.dtype),
            jax.ShapeDtypeStruct((1, list_width(slots)), jnp.int32),
        ),
        scratch_shapes=[
            pltpu.VMEM(codes.shape, codes.dtype),
            pltpu.VMEM(values.shape, values.dtype),
            pltpu.VMEM((TOGETHER * GROUP * PAIR, LANES), jnp.float32),
            pltpu.SemaphoreType.DMA((slots // (GROUP * TOGETHER),)),
            pltpu.SemaphoreType.DMA,
        ],
        cost_estimate=pl.CostEstimate(flops=0, bytes_accessed=4 * slots * BLK * BLK, transcendentals=0),
        compiler_params=pltpu.CompilerParams(vmem_limit_bytes=48 * MIB),
        name="relayout",
    )(count, codes, values)


def table_kernel(*refs):
    parts, table = refs[:-1], refs[-1]
    kind = table.dtype if parts[0].shape[0] % 16 == 0 else jnp.float32

    def build(q, carry):
        at = pl.ds(pl.multiple_of(q * LANES, LANES), LANES)
        x = [part[:, at].astype(kind) for part in parts]
        table[at, :] = jnp.concatenate(x + x, axis=0).T.astype(table.dtype)
        return carry

    lax.fori_loop(0, table.shape[0] // LANES, build, 0, unroll=4)


def make_table(parts):
    nodes = parts[0].shape[1]
    return pl.pallas_call(
        table_kernel,
        in_specs=[VMEM] * len(parts),
        out_specs=VMEM,
        out_shape=jax.ShapeDtypeStruct((nodes, LANES), jnp.bfloat16),
        compiler_params=pltpu.CompilerParams(vmem_limit_bytes=4 * MIB),
        cost_estimate=pl.CostEstimate(flops=1, bytes_accessed=1, transcendentals=0),
        name="table",
    )(*parts)


def product_kernel(trash, group, n_tables, words_ref, blocks_ref, *refs):
    tables, outs = refs[:n_tables], refs[n_tables:]
    pending, acc = outs[-1], outs[-2]
    bounds = words_ref.shape[1] - 8 + group
    start, end = words_ref[0, bounds], words_ref[0, bounds + 1]
    low = lax.broadcasted_iota(jnp.int32, (BLK, LANES), 1) < BLK
    acc[...] = jnp.zeros_like(acc)

    def add(first):
        for u in range(UNROLL):
            i = first + u
            word = words_ref[0, jnp.maximum(i, 0)]
            place = jnp.where((i >= start) & (i < end), word & ((1 << SOURCE_AT) - 1), trash)
            rows = pl.ds(pl.multiple_of(place * PAIR, PAIR), PAIR)
            acc[rows, :] = acc[rows, :] + pending[u * PAIR : (u + 1) * PAIR, :]

    def step(g, carry):
        first = start + g * UNROLL
        products = []
        for u in range(UNROLL):
            word = words_ref[0, first + u]
            block = blocks_ref[pl.ds(pl.multiple_of((word >> SLOT_AT) * PAIR, PAIR), PAIR), :]
            source = (word >> SOURCE_AT) & ((1 << (SLOT_AT - SOURCE_AT)) - 1)
            right = []
            for table in tables:
                part = table[pl.ds(pl.multiple_of(source * BLK, BLK), BLK), :]
                zero = jnp.zeros_like(part)
                right.append(jnp.concatenate([jnp.where(low, part, zero), jnp.where(low, zero, part)], axis=0))
            products.append(jnp.dot(block, jnp.concatenate(right, axis=1), preferred_element_type=jnp.float32))
        add(first - UNROLL)
        for u in range(UNROLL):
            pending[u * PAIR : (u + 1) * PAIR, :] = products[u]
        return carry

    groups = (end - start + (UNROLL - 1)) // UNROLL
    lax.fori_loop(0, groups, step, 0)
    add(start + (groups - 1) * UNROLL)
    if len(outs) > 2:
        outs[0][...] = acc[: trash * PAIR, :].astype(outs[0].dtype)


def product(group, words, blocks, tables, trash, sent):
    lanes = LANES * len(tables)
    full = jax.ShapeDtypeStruct(((trash + 1) * PAIR, lanes), jnp.float32)
    out = jax.ShapeDtypeStruct((trash * PAIR, lanes), jnp.bfloat16) if sent else full
    sums = [pltpu.VMEM(full.shape, full.dtype)] if sent else []
    return pl.pallas_call(
        functools.partial(product_kernel, trash, group, len(tables)),
        in_specs=[SMEM, VMEM] + [VMEM] * len(tables),
        out_specs=VMEM,
        out_shape=out,
        scratch_shapes=sums + [pltpu.VMEM((UNROLL * PAIR, lanes), jnp.float32)],
        compiler_params=pltpu.CompilerParams(vmem_limit_bytes=8 * MIB),
        cost_estimate=pl.CostEstimate(flops=1, bytes_accessed=1, transcendentals=0),
        name="product_send" if sent else "product_keep",
    )(words, blocks, *tables)


def add_kernel(keep_ref, got_ref, next_ref, send_ref):
    half = next_ref.shape[0]
    next_ref[...] = keep_ref[:half, :] + got_ref[:half, :].astype(jnp.float32)
    send_ref[...] = (keep_ref[half:, :] + got_ref[half:, :].astype(jnp.float32)).astype(send_ref.dtype)


def add_halves(keep, place, got):
    rows, lanes = got.shape
    half = (rows // 2, lanes)
    block = lambda shape, place: pl.BlockSpec(shape, lambda _: place)
    return pl.pallas_call(
        add_kernel,
        grid=(1,),
        in_specs=[block(got.shape, place), block(got.shape, (0, 0))],
        out_specs=(block(half, (0, 0)),) * 2,
        out_shape=(jax.ShapeDtypeStruct(half, jnp.float32), jax.ShapeDtypeStruct(half, jnp.bfloat16)),
        compiler_params=pltpu.CompilerParams(vmem_limit_bytes=8 * MIB),
        cost_estimate=pl.CostEstimate(flops=rows * lanes, bytes_accessed=MIB, transcendentals=0),
        name="add",
    )(keep, got)


def layer_kernel(index, counts, *refs):
    sums, (weight_ref, bias_ref, out_ref, wide, left, right) = list(refs[:-6]), refs[-6:]
    r = lax.axis_index("row")
    wide[...] = weight_ref[...].astype(jnp.float32)
    size = wide.shape[0] // (2 * len(index[0]))
    halves = []
    for pieces in index:
        rows = [wide[pl.ds(pl.multiple_of((r ^ i) * size, size), size), :] for i in pieces]
        halves.append(jnp.concatenate(rows, axis=0).astype(jnp.bfloat16))
    zero = jnp.zeros_like(halves[0])
    even = jnp.concatenate([halves[0], zero, halves[1], zero], axis=0)
    odd = jnp.concatenate([zero, halves[0], zero, halves[1]], axis=0)
    base = 0
    for count in counts:
        pairs = [(sums.pop(0), sums.pop(0)) for _ in range(count // 2)]
        aggregated = [(keep[...] + got[...].astype(jnp.float32)).astype(jnp.bfloat16) for keep, got in pairs]
        aggregated = jnp.concatenate(aggregated, axis=1)
        rows = aggregated.shape[0]
        for h, w in enumerate((even, odd)):
            hidden = jnp.dot(aggregated, w, preferred_element_type=jnp.float32) + bias_ref[...]
            hidden = jnp.maximum(hidden, 0.0)
            left[pl.ds(base + h, rows, stride=2), :] = hidden[:, :LANES]
            right[pl.ds(base + h, rows, stride=2), :] = hidden[:, LANES:]
        base += 2 * rows
    out_ref[:, :LANES] = left[...].astype(out_ref.dtype)
    out_ref[:, LANES:] = right[...].astype(out_ref.dtype)


def layer(index, sums, weight, bias):
    rows = sum(2 * part[0].shape[0] for part in sums)
    return pl.pallas_call(
        functools.partial(layer_kernel, index, [len(part) for part in sums]),
        out_shape=jax.ShapeDtypeStruct((rows, weight.shape[1]), jnp.bfloat16),
        scratch_shapes=[pltpu.VMEM(weight.shape, jnp.float32)] + [pltpu.VMEM((rows, LANES), jnp.float32)] * 2,
        compiler_params=pltpu.CompilerParams(vmem_limit_bytes=8 * MIB),
        name="layer",
    )(*[x for part in sums for x in part], weight, bias)


def exchange(x, axis, size, bit):
    return lax.ppermute(x, axis, [(i, i ^ (1 << bit)) for i in range(size)])


def shards(n_row, n_col, features, block_codes, block_count, block_values, weight, bias):
    top, col_axis_bits = log2(n_row) - 1, list(range(log2(n_col)))
    col_blocks = features.shape[0] // BLK
    row_total = col_blocks * n_col // n_row
    per = row_total // n_col

    z_first, x_first = tuple(col_axis_bits[1:] + col_axis_bits[:1]), tuple(col_axis_bits)
    chunks = ((per // 2, x_first), (per // 4, x_first), (per // 4, z_first))
    halves = [size * n_col // 2 for size, _ in chunks]

    def spread(pieces, index):
        for bit in range(top):
            pieces = pieces + [exchange(p, "row", n_row, bit) for p in pieces]
            index = index + [i ^ (1 << bit) for i in index]
        return pieces, index

    mine = features.T
    other = exchange(mine, "row", n_row, top)
    near, near_index = spread([mine], [0])
    blocks, words = relayout(chunks, log2(col_blocks), block_count, block_codes, block_values[0])

    tables = [make_table(near)]
    first = product(0, words, blocks, tables, halves[0], True)
    other, first = lax.optimization_barrier((other, first))
    far, far_index = spread([other], [1 << top])
    tables.append(make_table(far))
    sends = [(first, product(0, words, blocks, tables[1:], halves[0], True))]
    sends += [(product(k, words, blocks, tables, halves[k], True),) for k in (1, 2)]
    gots = [[exchange(s, "col", n_col, order[0]) for s in send] for send, (_, order) in zip(sends, chunks)]
    words, gots[0][0] = lax.optimization_barrier((words, gots[0][0]))
    kept = product(len(chunks), words, blocks, tables, sum(halves), False)
    kept_at = [sum(halves[:k]) // halves[k] for k in range(len(chunks))]
    parts = [[(kept, (at, f), got) for f, got in enumerate(g)] for at, g in zip(kept_at, gots)]
    for k in range(1, len(col_axis_bits)):
        for i, (_, order) in enumerate(chunks):
            sums = [add_halves(*part) for part in parts[i]]
            parts[i] = [(total, (0, 0), exchange(send, "col", n_col, order[k])) for total, send in sums]
    sums = [[x for keep, _, got in part for x in (keep, got)] for part in parts]
    return layer((near_index, far_index), sums, weight, bias[None, :])


def solution(mesh):
    in_specs = (P("col", "row"), P("row", "col"), P("row", "col"), P("row", "col", None), P(), P())
    out_specs = P(("row", "col"), None)
    body = functools.partial(shards, mesh.shape["row"], mesh.shape["col"])
    return jax.shard_map(body, mesh=mesh, in_specs=in_specs, out_specs=out_specs, check_vma=False)
```

profile of v0, /device:TPU:0, one launch (start us, length us, event | category | flops | bytes accessed | tf_op | source)
XLA Modules:
  0.0 47.4 jit_solution(15135007148893417114)
XLA Ops:
  0.0 0.5 collective-permute-start.1
  0.5 2.6 %collective-permute-start = (bf16[32,4096]{1,0:T(8,128)(2,1)}, bf16[32,4096]{1,0:T(8,128)(2,1)S(1)}, u32[]{:S(2)}, u32[]{:S(2)}) collective-permute-start(bf16[32,4096]{1,0:T(8,128)(2,1)} %bitcast.4), channel_id=1, source_target_pairs={{0,16},{8,24},{16,0},{24,8},{1,17},{9,25},{17,1},{25,9},{2,18},{10... | collective-permute-start | bytes 786440 | tf_op jit(solution)/shard_map/ppermute | solution.py:266
  3.7 0.7 %copy-done.2 = s32[1,384]{1,0:T(1,128)S(1)} copy-done((s32[1,384]{1,0:T(1,128)S(1)}, s32[1,384]{1,0:T(1,128)}, u32[]{:S(2)}) %copy-start.2) | copy-done | bytes 1560
  4.4 3.2 %relayout.1 = (bf16[12288,128]{1,0:T(8,128)(2,1)S(1)}, s32[1,512]{1,0:T(1,128)S(1)}) custom-call(s32[1,1]{1,0:T(1,128)S(6)} %copy.7.count_ref, s32[1,384]{1,0:T(1,128)S(1)} %copy-done.2, bf16[384,4096]{1,0:T(8,128)(2,1)} %bitcast.7), custom_call_target="tpu_custom_call" | custom-call | bytes 6291456 | tf_op jit(solution)/shard_map/relayout/pallas_call | solution.py:99
  7.6 0.7 %table.2.refs_0_ = bf16[4096,128]{1,0:T(8,128)(2,1)S(1)} custom-call(bf16[32,4096]{1,0:T(8,128)(2,1)S(1)} %bitcast.5, bf16[32,4096]{1,0:T(8,128)(2,1)S(1)} %collective-permute-done.1.refs_1_), custom_call_target="tpu_custom_call" | custom-call | flops 1 | bytes 1 | tf_op jit(solution)/shard_map/table/pallas_call | solution.py:135
  8.4 0.8 %product_send.4 = bf16[1024,128]{1,0:T(8,128)(2,1)S(1)} custom-call(s32[1,512]{1,0:T(1,128)S(1)} %get-tuple-element.30.words_ref, bf16[12288,128]{1,0:T(8,128)(2,1)S(1)} %get-tuple-element.28.blocks_ref, bf16[4096,128]{1,0:T(8,128)(2,1)S(1)} %table.2.refs_0_), custom_call_target="tpu_custom_call" | custom-call | flops 1 | bytes 1 | tf_op jit(solution)/shard_map/product_send/pallas_call | solution.py:192
  9.1 1.0 %collective-permute-done.refs_0_ = bf16[32,4096]{1,0:T(8,128)(2,1)S(1)} collective-permute-done((bf16[32,4096]{1,0:T(8,128)(2,1)}, bf16[32,4096]{1,0:T(8,128)(2,1)S(1)}, u32[]{:S(2)}, u32[]{:S(2)}) %collective-permute-start) | collective-permute-done | bytes 262176 | tf_op jit(solution)/shard_map/ppermute | solution.py:266
  10.2 1.3 %collective-permute-start.3 = (bf16[32,4096]{1,0:T(8,128)(2,1)S(1)}, bf16[32,4096]{1,0:T(8,128)(2,1)S(1)}, u32[]{:S(2)}, u32[]{:S(2)}) collective-permute-start(bf16[32,4096]{1,0:T(8,128)(2,1)S(1)} %collective-permute-done.refs_0_), channel_id=1, source_target_pairs={{0,8},{8,0},{16,24},{24,16},{1,9},{9,1},{17,25},{25,17},{2,10},{10... | collective-permute-start | bytes 786440 | tf_op jit(solution)/shard_map/ppermute | solution.py:266
  11.5 0.7 %collective-permute-start.2 = (bf16[1024,128]{1,0:T(8,128)(2,1)S(1)}, bf16[1024,128]{1,0:T(8,128)(2,1)S(1)}, u32[]{:S(2)}, u32[]{:S(2)}) collective-permute-start(bf16[1024,128]{1,0:T(8,128)(2,1)S(1)} %product_send.4), channel_id=1, source_target_pairs={{0,1},{1,0},{2,3},{3,2},{4,5},{5,4},{6,7},{7,6},{8,9},{9,8},{10,11... | collective-permute-start | bytes 786440 | tf_op jit(solution)/shard_map/ppermute | solution.py:266
  12.2 0.4 collective-permute-done.3.refs_1_
  12.6 0.7 %table.3.refs_1_.refs_0_ = bf16[4096,128]{1,0:T(8,128)(2,1)S(1)} custom-call(bf16[32,4096]{1,0:T(8,128)(2,1)S(1)} %collective-permute-done.refs_0_, bf16[32,4096]{1,0:T(8,128)(2,1)S(1)} %collective-permute-done.3.refs_1_), custom_call_target="tpu_custom_call" | custom-call | flops 1 | bytes 1 | tf_op jit(solution)/shard_map/table/pallas_call | solution.py:135
  13.4 0.8 %product_send.7 = bf16[512,256]{1,0:T(8,128)(2,1)S(1)} custom-call(s32[1,512]{1,0:T(1,128)S(1)} %get-tuple-element.30.words_ref, bf16[12288,128]{1,0:T(8,128)(2,1)S(1)} %get-tuple-element.28.blocks_ref, bf16[4096,128]{1,0:T(8,128)(2,1)S(1)} %table.2.refs_0_, bf16[4096,128]{1,0:T(8,128)(2,1)S(1)} %table.3.refs_1_.refs_0_), custom_call_target="tpu_custom_call" | custom-call | flops 1 | bytes 1 | tf_op jit(solution)/shard_map/product_send/pallas_call | solution.py:192
  14.1 2.4 %collective-permute-start.12 = (bf16[512,256]{1,0:T(8,128)(2,1)S(1)}, bf16[512,256]{1,0:T(8,128)(2,1)S(1)}, u32[]{:S(2)}, u32[]{:S(2)}) collective-permute-start(bf16[512,256]{1,0:T(8,128)(2,1)S(1)} %product_send.7), channel_id=1, source_target_pairs={{0,2},{1,3},{2,0},{3,1},{4,6},{5,7},{6,4},{7,5},{8,10},{9,11},{10,... | collective-permute-start | bytes 786440 | tf_op jit(solution)/shard_map/ppermute | solution.py:266
  16.5 1.0 %product_send.6 = bf16[512,256]{1,0:T(8,128)(2,1)S(1)} custom-call(s32[1,512]{1,0:T(1,128)S(1)} %get-tuple-element.30.words_ref, bf16[12288,128]{1,0:T(8,128)(2,1)S(1)} %get-tuple-element.28.blocks_ref, bf16[4096,128]{1,0:T(8,128)(2,1)S(1)} %table.2.refs_0_, bf16[4096,128]{1,0:T(8,128)(2,1)S(1)} %table.3.refs_1_.refs_0_), custom_call_target="tpu_custom_call" | custom-call | flops 1 | bytes 1 | tf_op jit(solution)/shard_map/product_send/pallas_call | solution.py:192
  17.6 0.9 %collective-permute-start.9 = (bf16[512,256]{1,0:T(8,128)(2,1)S(1)}, bf16[512,256]{1,0:T(8,128)(2,1)S(1)}, u32[]{:S(2)}, u32[]{:S(2)}) collective-permute-start(bf16[512,256]{1,0:T(8,128)(2,1)S(1)} %product_send.6), channel_id=1, source_target_pairs={{0,1},{1,0},{2,3},{3,2},{4,5},{5,4},{6,7},{7,6},{8,9},{9,8},{10,11... | collective-permute-start | bytes 786440 | tf_op jit(solution)/shard_map/ppermute | solution.py:266
  18.5 0.7 %product_send.5 = bf16[1024,128]{1,0:T(8,128)(2,1)S(1)} custom-call(s32[1,512]{1,0:T(1,128)S(1)} %get-tuple-element.30.words_ref, bf16[12288,128]{1,0:T(8,128)(2,1)S(1)} %get-tuple-element.28.blocks_ref, bf16[4096,128]{1,0:T(8,128)(2,1)S(1)} %table.3.refs_1_.refs_0_), custom_call_target="tpu_custom_call" | custom-call | flops 1 | bytes 1 | tf_op jit(solution)/shard_map/product_send/pallas_call | solution.py:192
  19.2 2.5 %collective-permute-start.6 = (bf16[1024,128]{1,0:T(8,128)(2,1)S(1)}, bf16[1024,128]{1,0:T(8,128)(2,1)S(1)}, u32[]{:S(2)}, u32[]{:S(2)}) collective-permute-start(bf16[1024,128]{1,0:T(8,128)(2,1)S(1)} %product_send.5), channel_id=1, source_target_pairs={{0,1},{1,0},{2,3},{3,2},{4,5},{5,4},{6,7},{7,6},{8,9},{9,8},{10,11... | collective-permute-start | bytes 786440 | tf_op jit(solution)/shard_map/ppermute | solution.py:266
  21.8 1.1 %product_keep.1.keep_ref = f32[2080,256]{1,0:T(8,128)S(1)} custom-call(s32[1,512]{1,0:T(1,128)S(1)} %get-tuple-element.30.words_ref, bf16[12288,128]{1,0:T(8,128)(2,1)S(1)} %get-tuple-element.28.blocks_ref, bf16[4096,128]{1,0:T(8,128)(2,1)S(1)} %table.2.refs_0_, bf16[4096,128]{1,0:T(8,128)(2,1)S(1)} %table.3.refs_1_.refs_0_), custom_call_target="tpu_custom_call" | custom-call | flops 1 | bytes 1 | tf_op jit(solution)/shard_map/product_keep/pallas_call | solution.py:192
  22.9 3.4 %collective-permute-start.4 = (bf16[512,128]{1,0:T(8,128)(2,1)S(1)}, bf16[512,128]{1,0:T(8,128)(2,1)S(1)}, u32[]{:S(2)}, u32[]{:S(2)}) collective-permute-start(bf16[512,128]{1,0:T(8,128)(2,1)S(1)} %get-tuple-element.34), channel_id=1, source_target_pairs={{0,2},{1,3},{2,0},{3,1},{4,6},{5,7},{6,4},{7,5},{8,10},{9,11},{10,... | collective-permute-start | bytes 393224 | tf_op jit(solution)/shard_map/ppermute | solution.py:266
  26.4 2.1 %collective-permute-start.13 = (bf16[256,256]{1,0:T(8,128)(2,1)S(1)}, bf16[256,256]{1,0:T(8,128)(2,1)S(1)}, u32[]{:S(2)}, u32[]{:S(2)}) collective-permute-start(bf16[256,256]{1,0:T(8,128)(2,1)S(1)} %get-tuple-element.46), channel_id=1, source_target_pairs={{0,4},{1,5},{2,6},{3,7},{4,0},{5,1},{6,2},{7,3},{8,12},{9,13},{10,... | collective-permute-start | bytes 393224 | tf_op jit(solution)/shard_map/ppermute | solution.py:266
  28.6 0.1 collective-permute-start.10
  28.6 2.4 %collective-permute-done.6.got_ref = bf16[1024,128]{1,0:T(8,128)(2,1)S(1)} collective-permute-done((bf16[1024,128]{1,0:T(8,128)(2,1)S(1)}, bf16[1024,128]{1,0:T(8,128)(2,1)S(1)}, u32[]{:S(2)}, u32[]{:S(2)}) %collective-permute-start.6) | collective-permute-done | bytes 262176 | tf_op jit(solution)/shard_map/ppermute | solution.py:266
  31.1 1.3 %collective-permute-start.7 = (bf16[512,128]{1,0:T(8,128)(2,1)S(1)}, bf16[512,128]{1,0:T(8,128)(2,1)S(1)}, u32[]{:S(2)}, u32[]{:S(2)}) collective-permute-start(bf16[512,128]{1,0:T(8,128)(2,1)S(1)} %get-tuple-element.38), channel_id=1, source_target_pairs={{0,2},{1,3},{2,0},{3,1},{4,6},{5,7},{6,4},{7,5},{8,10},{9,11},{10,... | collective-permute-start | bytes 393224 | tf_op jit(solution)/shard_map/ppermute | solution.py:266
  32.5 2.6 %collective-permute-start.5 = (bf16[256,128]{1,0:T(8,128)(2,1)S(1)}, bf16[256,128]{1,0:T(8,128)(2,1)S(1)}, u32[]{:S(2)}, u32[]{:S(2)}) collective-permute-start(bf16[256,128]{1,0:T(8,128)(2,1)S(1)} %get-tuple-element.36), channel_id=1, source_target_pairs={{0,4},{1,5},{2,6},{3,7},{4,0},{5,1},{6,2},{7,3},{8,12},{9,13},{10,... | collective-permute-start | bytes 196616 | tf_op jit(solution)/shard_map/ppermute | solution.py:266
  35.1 1.2 %collective-permute-start.14 = (bf16[128,256]{1,0:T(8,128)(2,1)S(1)}, bf16[128,256]{1,0:T(8,128)(2,1)S(1)}, u32[]{:S(2)}, u32[]{:S(2)}) collective-permute-start(bf16[128,256]{1,0:T(8,128)(2,1)S(1)} %get-tuple-element.48), channel_id=1, source_target_pairs={{0,1},{1,0},{2,3},{3,2},{4,5},{5,4},{6,7},{7,6},{8,9},{9,8},{10,11... | collective-permute-start | bytes 196616 | tf_op jit(solution)/shard_map/ppermute | solution.py:266
  36.3 0.7 %collective-permute-done.10.got_ref = bf16[256,256]{1,0:T(8,128)(2,1)S(1)} collective-permute-done((bf16[256,256]{1,0:T(8,128)(2,1)S(1)}, bf16[256,256]{1,0:T(8,128)(2,1)S(1)}, u32[]{:S(2)}, u32[]{:S(2)}) %collective-permute-start.10) | collective-permute-done | bytes 131104 | tf_op jit(solution)/shard_map/ppermute | solution.py:266
  37.0 0.9 %collective-permute-start.11 = (bf16[128,256]{1,0:T(8,128)(2,1)S(1)}, bf16[128,256]{1,0:T(8,128)(2,1)S(1)}, u32[]{:S(2)}, u32[]{:S(2)}) collective-permute-start(bf16[128,256]{1,0:T(8,128)(2,1)S(1)} %get-tuple-element.44), channel_id=1, source_target_pairs={{0,4},{1,5},{2,6},{3,7},{4,0},{5,1},{6,2},{7,3},{8,12},{9,13},{10,... | collective-permute-start | bytes 196616 | tf_op jit(solution)/shard_map/ppermute | solution.py:266
  38.0 2.3 %collective-permute-done.7.got_ref = bf16[512,128]{1,0:T(8,128)(2,1)S(1)} collective-permute-done((bf16[512,128]{1,0:T(8,128)(2,1)S(1)}, bf16[512,128]{1,0:T(8,128)(2,1)S(1)}, u32[]{:S(2)}, u32[]{:S(2)}) %collective-permute-start.7) | collective-permute-done | bytes 131104 | tf_op jit(solution)/shard_map/ppermute | solution.py:266
  40.3 0.4 collective-permute-start.8
  40.8 4.2 %collective-permute-done.11.refs_5_ = bf16[128,256]{1,0:T(8,128)(2,1)S(1)} collective-permute-done((bf16[128,256]{1,0:T(8,128)(2,1)S(1)}, bf16[128,256]{1,0:T(8,128)(2,1)S(1)}, u32[]{:S(2)}, u32[]{:S(2)}) %collective-permute-start.11) | collective-permute-done | bytes 65568 | tf_op jit(solution)/shard_map/ppermute | solution.py:266
  44.9 1.3 %collective-permute-done.8.refs_3_ = bf16[256,128]{1,0:T(8,128)(2,1)S(1)} collective-permute-done((bf16[256,128]{1,0:T(8,128)(2,1)S(1)}, bf16[256,128]{1,0:T(8,128)(2,1)S(1)}, u32[]{:S(2)}, u32[]{:S(2)}) %collective-permute-start.8) | collective-permute-done | bytes 65568 | tf_op jit(solution)/shard_map/ppermute | solution.py:266
  46.2 1.2 %layer.1 = bf16[1024,256]{1,0:T(8,128)(2,1)} custom-call(f32[256,128]{1,0:T(8,128)S(1)} %get-tuple-element.35.refs_0_, bf16[256,128]{1,0:T(8,128)(2,1)S(1)} %collective-permute-done.5.refs_1_, f32[256,128]{1,0:T(8,128)S(1)} %get-tuple-element.39.refs_2_, bf16[256,128]{1,0:T(8,128)(2,1)S(1)} %collective-permute-done.8.refs_3_, ...), custom_call_target="tpu_custom_call" | custom-call | tf_op jit(solution)/shard_map/layer/pallas_call | solution.py:256
  (23 shorter events, 0.4 us)
Async XLA Ops:
  0.0 7.6 %copy-start = (bf16[4096,32]{0,1:T(8,128)(2,1)S(1)}, bf16[4096,32]{0,1:T(8,128)(2,1)}, u32[]{:S(2)}) copy-start(bf16[4096,32]{0,1:T(8,128)(2,1)} %param.6) | copy-start | bytes 786436
  0.0 7.6 %collective-permute-start.1 = (bf16[32,4096]{1,0:T(8,128)(2,1)}, bf16[32,4096]{1,0:T(8,128)(2,1)S(1)}, u32[]{:S(2)}, u32[]{:S(2)}) collective-permute-start(bf16[32,4096]{1,0:T(8,128)(2,1)} %bitcast.3), channel_id=1, source_target_pairs={{0,8},{8,0},{16,24},{24,16},{1,9},{9,1},{17,25},{25,17},{2,10},{10... | collective-permute-start | bytes 786440 | tf_op jit(solution)/shard_map/ppermute | solution.py:266
  0.5 9.7 %collective-permute-start = (bf16[32,4096]{1,0:T(8,128)(2,1)}, bf16[32,4096]{1,0:T(8,128)(2,1)S(1)}, u32[]{:S(2)}, u32[]{:S(2)}) collective-permute-start(bf16[32,4096]{1,0:T(8,128)(2,1)} %bitcast.4), channel_id=1, source_target_pairs={{0,16},{8,24},{16,0},{24,8},{1,17},{9,25},{17,1},{25,9},{2,18},{10... | collective-permute-start | bytes 786440 | tf_op jit(solution)/shard_map/ppermute | solution.py:266
  3.7 0.7 %copy-start.2 = (s32[1,384]{1,0:T(1,128)S(1)}, s32[1,384]{1,0:T(1,128)}, u32[]{:S(2)}) copy-start(s32[1,384]{1,0:T(1,128)} %codes_hbm.1) | copy-start | bytes 4612
  10.2 2.5 %collective-permute-start.3 = (bf16[32,4096]{1,0:T(8,128)(2,1)S(1)}, bf16[32,4096]{1,0:T(8,128)(2,1)S(1)}, u32[]{:S(2)}, u32[]{:S(2)}) collective-permute-start(bf16[32,4096]{1,0:T(8,128)(2,1)S(1)} %collective-permute-done.refs_0_), channel_id=1, source_target_pairs={{0,8},{8,0},{16,24},{24,16},{1,9},{9,1},{17,25},{25,17},{2,10},{10... | collective-permute-start | bytes 786440 | tf_op jit(solution)/shard_map/ppermute | solution.py:266
  11.5 10.3 %collective-permute-start.2 = (bf16[1024,128]{1,0:T(8,128)(2,1)S(1)}, bf16[1024,128]{1,0:T(8,128)(2,1)S(1)}, u32[]{:S(2)}, u32[]{:S(2)}) collective-permute-start(bf16[1024,128]{1,0:T(8,128)(2,1)S(1)} %product_send.4), channel_id=1, source_target_pairs={{0,1},{1,0},{2,3},{3,2},{4,5},{5,4},{6,7},{7,6},{8,9},{9,8},{10,11... | collective-permute-start | bytes 786440 | tf_op jit(solution)/shard_map/ppermute | solution.py:266
  14.1 12.2 %collective-permute-start.12 = (bf16[512,256]{1,0:T(8,128)(2,1)S(1)}, bf16[512,256]{1,0:T(8,128)(2,1)S(1)}, u32[]{:S(2)}, u32[]{:S(2)}) collective-permute-start(bf16[512,256]{1,0:T(8,128)(2,1)S(1)} %product_send.7), channel_id=1, source_target_pairs={{0,2},{1,3},{2,0},{3,1},{4,6},{5,7},{6,4},{7,5},{8,10},{9,11},{10,... | collective-permute-start | bytes 786440 | tf_op jit(solution)/shard_map/ppermute | solution.py:266
  17.6 10.9 %collective-permute-start.9 = (bf16[512,256]{1,0:T(8,128)(2,1)S(1)}, bf16[512,256]{1,0:T(8,128)(2,1)S(1)}, u32[]{:S(2)}, u32[]{:S(2)}) collective-permute-start(bf16[512,256]{1,0:T(8,128)(2,1)S(1)} %product_send.6), channel_id=1, source_target_pairs={{0,1},{1,0},{2,3},{3,2},{4,5},{5,4},{6,7},{7,6},{8,9},{9,8},{10,11... | collective-permute-start | bytes 786440 | tf_op jit(solution)/shard_map/ppermute | solution.py:266
  19.2 11.8 %collective-permute-start.6 = (bf16[1024,128]{1,0:T(8,128)(2,1)S(1)}, bf16[1024,128]{1,0:T(8,128)(2,1)S(1)}, u32[]{:S(2)}, u32[]{:S(2)}) collective-permute-start(bf16[1024,128]{1,0:T(8,128)(2,1)S(1)} %product_send.5), channel_id=1, source_target_pairs={{0,1},{1,0},{2,3},{3,2},{4,5},{5,4},{6,7},{7,6},{8,9},{9,8},{10,11... | collective-permute-start | bytes 786440 | tf_op jit(solution)/shard_map/ppermute | solution.py:266
  22.9 9.5 %collective-permute-start.4 = (bf16[512,128]{1,0:T(8,128)(2,1)S(1)}, bf16[512,128]{1,0:T(8,128)(2,1)S(1)}, u32[]{:S(2)}, u32[]{:S(2)}) collective-permute-start(bf16[512,128]{1,0:T(8,128)(2,1)S(1)} %get-tuple-element.34), channel_id=1, source_target_pairs={{0,2},{1,3},{2,0},{3,1},{4,6},{5,7},{6,4},{7,5},{8,10},{9,11},{10,... | collective-permute-start | bytes 393224 | tf_op jit(solution)/shard_map/ppermute | solution.py:266
  26.4 19.8 %copy-start.1 = (bf16[128,256]{1,0:T(8,128)(2,1)S(1)}, bf16[128,256]{1,0:T(8,128)(2,1)}, u32[]{:S(2)}) copy-start(bf16[128,256]{1,0:T(8,128)(2,1)} %refs_8_.1) | copy-start | bytes 196612
  26.4 19.8 %copy-start.3 = (f32[256]{0:T(256)S(1)}, f32[256]{0:T(256)}, u32[]{:S(2)}) copy-start(f32[256]{0:T(256)} %param.11) | copy-start | bytes 3076
  26.4 8.7 %collective-permute-start.13 = (bf16[256,256]{1,0:T(8,128)(2,1)S(1)}, bf16[256,256]{1,0:T(8,128)(2,1)S(1)}, u32[]{:S(2)}, u32[]{:S(2)}) collective-permute-start(bf16[256,256]{1,0:T(8,128)(2,1)S(1)} %get-tuple-element.46), channel_id=1, source_target_pairs={{0,4},{1,5},{2,6},{3,7},{4,0},{5,1},{6,2},{7,3},{8,12},{9,13},{10,... | collective-permute-start | bytes 393224 | tf_op jit(solution)/shard_map/ppermute | solution.py:266
  28.6 8.4 %collective-permute-start.10 = (bf16[256,256]{1,0:T(8,128)(2,1)S(1)}, bf16[256,256]{1,0:T(8,128)(2,1)S(1)}, u32[]{:S(2)}, u32[]{:S(2)}) collective-permute-start(bf16[256,256]{1,0:T(8,128)(2,1)S(1)} %get-tuple-element.42), channel_id=1, source_target_pairs={{0,2},{1,3},{2,0},{3,1},{4,6},{5,7},{6,4},{7,5},{8,10},{9,11},{10,... | collective-permute-start | bytes 393224 | tf_op jit(solution)/shard_map/ppermute | solution.py:266
  31.1 9.2 %collective-permute-start.7 = (bf16[512,128]{1,0:T(8,128)(2,1)S(1)}, bf16[512,128]{1,0:T(8,128)(2,1)S(1)}, u32[]{:S(2)}, u32[]{:S(2)}) collective-permute-start(bf16[512,128]{1,0:T(8,128)(2,1)S(1)} %get-tuple-element.38), channel_id=1, source_target_pairs={{0,2},{1,3},{2,0},{3,1},{4,6},{5,7},{6,4},{7,5},{8,10},{9,11},{10,... | collective-permute-start | bytes 393224 | tf_op jit(solution)/shard_map/ppermute | solution.py:266
  32.5 8.3 %collective-permute-start.5 = (bf16[256,128]{1,0:T(8,128)(2,1)S(1)}, bf16[256,128]{1,0:T(8,128)(2,1)S(1)}, u32[]{:S(2)}, u32[]{:S(2)}) collective-permute-start(bf16[256,128]{1,0:T(8,128)(2,1)S(1)} %get-tuple-element.36), channel_id=1, source_target_pairs={{0,4},{1,5},{2,6},{3,7},{4,0},{5,1},{6,2},{7,3},{8,12},{9,13},{10,... | collective-permute-start | bytes 196616 | tf_op jit(solution)/shard_map/ppermute | solution.py:266
  35.1 5.6 %collective-permute-start.14 = (bf16[128,256]{1,0:T(8,128)(2,1)S(1)}, bf16[128,256]{1,0:T(8,128)(2,1)S(1)}, u32[]{:S(2)}, u32[]{:S(2)}) collective-permute-start(bf16[128,256]{1,0:T(8,128)(2,1)S(1)} %get-tuple-element.48), channel_id=1, source_target_pairs={{0,1},{1,0},{2,3},{3,2},{4,5},{5,4},{6,7},{7,6},{8,9},{9,8},{10,11... | collective-permute-start | bytes 196616 | tf_op jit(solution)/shard_map/ppermute | solution.py:266
  37.0 7.9 %collective-permute-start.11 = (bf16[128,256]{1,0:T(8,128)(2,1)S(1)}, bf16[128,256]{1,0:T(8,128)(2,1)S(1)}, u32[]{:S(2)}, u32[]{:S(2)}) collective-permute-start(bf16[128,256]{1,0:T(8,128)(2,1)S(1)} %get-tuple-element.44), channel_id=1, source_target_pairs={{0,4},{1,5},{2,6},{3,7},{4,0},{5,1},{6,2},{7,3},{8,12},{9,13},{10,... | collective-permute-start | bytes 196616 | tf_op jit(solution)/shard_map/ppermute | solution.py:266
  40.3 5.9 %collective-permute-start.8 = (bf16[256,128]{1,0:T(8,128)(2,1)S(1)}, bf16[256,128]{1,0:T(8,128)(2,1)S(1)}, u32[]{:S(2)}, u32[]{:S(2)}) collective-permute-start(bf16[256,128]{1,0:T(8,128)(2,1)S(1)} %get-tuple-element.40), channel_id=1, source_target_pairs={{0,4},{1,5},{2,6},{3,7},{4,0},{5,1},{6,2},{7,3},{8,12},{9,13},{10,... | collective-permute-start | bytes 196616 | tf_op jit(solution)/shard_map/ppermute | solution.py:266
where the time goes:
time: 47.3 us; the launch traced here: 47.4 us
  starting transfers between devices  23 us (49%)
  waiting for transfers between devices  12.3 us (26%)
  Pallas kernels  10.6 us (22%)
  between operations  0.78 us (2%)
  local copies, waits for them, and re-layouts  0.69 us (1%)
    ppermute x15, starting transfers between devices, exchange(): return lax.ppermute(x, axis, [(i, i ^ 1 << bit) for i in range(size)])  23 us
    ppermute x15, waiting for transfers between devices, exchange(): return lax.ppermute(x, axis, [(i, i ^ 1 << bit) for i in range(size)])  12.3 us
    pallas_call x5, Pallas kernels, product(): pl.pallas_call(functools.partial(product_kernel, trash, group, len(tables...  4.39 us
    pallas_call x1, Pallas kernels, relayout(): pl.pallas_call(functools.partial(relayout_kernel, chunks, col_bits), in_s...  3.24 us
    pallas_call x2, Pallas kernels, make_table(): pl.pallas_call(table_kernel, in_specs=[VMEM] * len(parts), out_specs=VMEM...  1.49 us
    pallas_call x1, Pallas kernels, layer(): pl.pallas_call(functools.partial(layer_kernel, index, [len(part) for part...  1.19 us
  transfers between devices with their start and end apart: 15, of which 7 were waited for; matrix products, arithmetic and copies ran while one was open for 0% of the time, Pallas kernels for 20%

commit v1 on v0

--- a/solution.py
+++ b/solution.py
@@ -223,21 +223,9 @@
     )(keep, got)
 
 
-def layer_kernel(index, counts, *refs):
-    sums, (weight_ref, bias_ref, out_ref, wide, left, right) = list(refs[:-6]), refs[-6:]
-    r = lax.axis_index("row")
-    wide[...] = weight_ref[...].astype(jnp.float32)
-    size = wide.shape[0] // (2 * len(index[0]))
-    halves = []
-    for pieces in index:
-        rows = [wide[pl.ds(pl.multiple_of((r ^ i) * size, size), size), :] for i in pieces]
-        halves.append(jnp.concatenate(rows, axis=0).astype(jnp.bfloat16))
-    zero = jnp.zeros_like(halves[0])
-    even = jnp.concatenate([halves[0], zero, halves[1], zero], axis=0)
-    odd = jnp.concatenate([zero, halves[0], zero, halves[1]], axis=0)
+def layer_rows(sums, even, odd, bias_ref, out_hbm, first, left, right, result, sem):
     base = 0
-    for count in counts:
-        pairs = [(sums.pop(0), sums.pop(0)) for _ in range(count // 2)]
+    for pairs in sums:
         aggregated = [(keep[...] + got[...].astype(jnp.float32)).astype(jnp.bfloat16) for keep, got in pairs]
         aggregated = jnp.concatenate(aggregated, axis=1)
         rows = aggregated.shape[0]
@@ -247,19 +235,76 @@
             left[pl.ds(base + h, rows, stride=2), :] = hidden[:, :LANES]
             right[pl.ds(base + h, rows, stride=2), :] = hidden[:, LANES:]
         base += 2 * rows
-    out_ref[:, :LANES] = left[...].astype(out_ref.dtype)
-    out_ref[:, LANES:] = right[...].astype(out_ref.dtype)
+    result[:, :LANES] = left[...].astype(result.dtype)
+    result[:, LANES:] = right[...].astype(result.dtype)
+    copy = pltpu.make_async_copy(result, out_hbm.at[pl.ds(first, base)], sem)
+    copy.start()
+    copy.wait()
+
+
+def grouped(refs, counts):
+    refs, groups = list(refs), []
+    for count in counts:
+        groups.append([(refs.pop(0), refs.pop(0)) for _ in range(count)])
+    return groups
+
+
+def first_layer_kernel(index, counts, first, *refs):
+    sums = grouped(refs, counts)
+    weight_ref, bias_ref, out_hbm, even_ref, odd_ref, wide, *scratch = refs[2 * sum(counts) :]
+    r = lax.axis_index("row")
+    wide[...] = weight_ref[...].astype(jnp.float32)
+    size = wide.shape[0] // (2 * len(index[0]))
+    halves = []
+    for pieces in index:
+        rows = [wide[pl.ds(pl.multiple_of((r ^ i) * size, size), size), :] for i in pieces]
+        halves.append(jnp.concatenate(rows, axis=0).astype(jnp.bfloat16))
+    zero = jnp.zeros_like(halves[0])
+    even_ref[...] = jnp.concatenate([halves[0], zero, halves[1], zero], axis=0)
+    odd_ref[...] = jnp.concatenate([zero, halves[0], zero, halves[1]], axis=0)
+    layer_rows(sums, even_ref[...], odd_ref[...], bias_ref, out_hbm, first, *scratch)
+
+
+def last_layer_kernel(counts, first, *refs):
+    sums = grouped(refs, counts)
+    even_ref, odd_ref, bias_ref, _, out_hbm, *scratch = refs[2 * sum(counts) :]
+    layer_rows(sums, even_ref[...], odd_ref[...], bias_ref, out_hbm, first, *scratch)
+
+
+def layer_scratch(rows, lanes):
+    wide = [pltpu.VMEM((rows, LANES), jnp.float32)] * 2
+    return wide + [pltpu.VMEM((rows, lanes), jnp.bfloat16), pltpu.SemaphoreType.DMA]
 
 
 def layer(index, sums, weight, bias):
-    rows = sum(2 * part[0].shape[0] for part in sums)
-    return pl.pallas_call(
-        functools.partial(layer_kernel, index, [len(part) for part in sums]),
-        out_shape=jax.ShapeDtypeStruct((rows, weight.shape[1]), jnp.bfloat16),
-        scratch_shapes=[pltpu.VMEM(weight.shape, jnp.float32)] + [pltpu.VMEM((rows, LANES), jnp.float32)] * 2,
-        compiler_params=pltpu.CompilerParams(vmem_limit_bytes=8 * MIB),
-        name="layer",
-    )(*[x for part in sums for x in part], weight, bias)
+    counts = [len(part) // 2 for part in sums]
+    sizes = [2 * part[0].shape[0] for part in sums]
+    lanes = weight.shape[1]
+    anywhere = pl.BlockSpec(memory_space=pl.ANY)
+    params = pltpu.CompilerParams(vmem_limit_bytes=8 * MIB)
+    shape = jax.ShapeDtypeStruct((sum(sizes), lanes), jnp.bfloat16)
+    expanded = jax.ShapeDtypeStruct((2 * LANES, lanes), jnp.bfloat16)
+    flat = [x for part in sums[1:] for x in part]
+    out, even, odd = pl.pallas_call(
+        functools.partial(first_layer_kernel, index, counts[1:], sizes[0]),
+        in_specs=[VMEM] * (len(flat) + 2),
+        out_specs=(anywhere, VMEM, VMEM),
+        out_shape=(shape, expanded, expanded),
+        scratch_shapes=[pltpu.VMEM(weight.shape, jnp.float32)] + layer_scratch(sum(sizes[1:]), lanes),
+        compiler_params=params,
+        name="layer_first",
+    )(*flat, weight, bias)
+    flat, out = lax.optimization_barrier((sums[0], out))
+    return pl.pallas_call(
+        functools.partial(last_layer_kernel, counts[:1], 0),
+        in_specs=[VMEM] * (len(flat) + 3) + [anywhere],
+        out_specs=anywhere,
+        out_shape=shape,
+        input_output_aliases={len(flat) + 3: 0},
+        scratch_shapes=layer_scratch(sizes[0], lanes),
+        compiler_params=params,
+        name="layer_last",
+    )(*flat, even, odd, bias, out)
 
 
 def exchange(x, axis, size, bit):

time: 47.3 us -> 46.6 us (0.985)
  starting transfers between devices: 23 us -> 22.4 us
  Pallas kernels: 10.6 us -> 11.1 us
  waiting for transfers between devices: 12.3 us -> 11.8 us
    pallas_call x1 -> x2, Pallas kernels: 1.19 us -> 1.97 us  [the longest x1 1 us: layer(): pl.pallas_call(functools.partial(first_layer_kernel, index, counts[1:], s...]
    ppermute x15, starting transfers between devices: 23 us -> 22.4 us  [exchange(): return lax.ppermute(x, axis, [(i, i ^ 1 << bit) for i in range(size)])]
    ppermute x15, waiting for transfers between devices: 12.3 us -> 11.8 us  [exchange(): return lax.ppermute(x, axis, [(i, i ^ 1 << bit) for i in range(size)])]
  transfers between devices with their start and end apart: 15 -> 15, of which waited for: 7 -> 10; matrix products, arithmetic and copies ran while one was open for 0% -> 0% of each run, Pallas kernels for 20% -> 22%
where the time goes in v1:
time: 46.6 us; the launch traced here: 46.8 us
  starting transfers between devices  22.4 us (48%)
  waiting for transfers between devices  11.8 us (25%)
  Pallas kernels  11.1 us (24%)
  between operations  0.8 us (2%)
  local copies, waits for them, and re-layouts  0.69 us (1%)
    ppermute x15, starting transfers between devices, exchange(): return lax.ppermute(x, axis, [(i, i ^ 1 << bit) for i in range(size)])  22.4 us
    ppermute x15, waiting for transfers between devices, exchange(): return lax.ppermute(x, axis, [(i, i ^ 1 << bit) for i in range(size)])  11.8 us
    pallas_call x5, Pallas kernels, product(): pl.pallas_call(functools.partial(product_kernel, trash, group, len(tables...  4.12 us
    pallas_call x1, Pallas kernels, relayout(): pl.pallas_call(functools.partial(relayout_kernel, chunks, col_bits), in_s...  3.24 us
    pallas_call x2, Pallas kernels, make_table(): pl.pallas_call(table_kernel, in_specs=[VMEM] * len(parts), out_specs=VMEM...  1.49 us
    pallas_call x1, Pallas kernels, layer(): pl.pallas_call(functools.partial(first_layer_kernel, index, counts[1:], s...  1 us
    pallas_call x1, Pallas kernels, layer(): pl.pallas_call(functools.partial(last_layer_kernel, counts[:1], 0), in_sp...  0.98 us
  transfers between devices with their start and end apart: 15, of which 10 were waited for; matrix products, arithmetic and copies ran while one was open for 0% of the time, Pallas kernels for 22%

profile of v1, /device:TPU:0, one launch (start us, length us, event | category | flops | bytes accessed | tf_op | source)
XLA Modules:
  0.0 46.8 jit_solution(4868511042039051247)
XLA Ops:
  0.5 2.6 %collective-permute-start = (bf16[32,4096]{1,0:T(8,128)(2,1)}, bf16[32,4096]{1,0:T(8,128)(2,1)S(1)}, u32[]{:S(2)}, u32[]{:S(2)}) collective-permute-start(bf16[32,4096]{1,0:T(8,128)(2,1)} %bitcast.4), channel_id=1, source_target_pairs={{0,16},{8,24},{16,0},{24,8},{1,17},{9,25},{17,1},{25,9},{2,18},{10... | collective-permute-start | bytes 786440 | tf_op jit(solution)/shard_map/ppermute | solution.py:311
  3.7 0.7 %copy-done.3 = s32[1,384]{1,0:T(1,128)S(1)} copy-done((s32[1,384]{1,0:T(1,128)S(1)}, s32[1,384]{1,0:T(1,128)}, u32[]{:S(2)}) %copy-start.3) | copy-done | bytes 1560
  4.4 3.2 %relayout.1 = (bf16[12288,128]{1,0:T(8,128)(2,1)S(1)}, s32[1,512]{1,0:T(1,128)S(1)}) custom-call(s32[1,1]{1,0:T(1,128)S(6)} %copy.9.count_ref, s32[1,384]{1,0:T(1,128)S(1)} %copy-done.3, bf16[384,4096]{1,0:T(8,128)(2,1)} %bitcast.8), custom_call_target="tpu_custom_call" | custom-call | bytes 6291456 | tf_op jit(solution)/shard_map/relayout/pallas_call | solution.py:99
  7.6 0.7 %table.2.refs_0_ = bf16[4096,128]{1,0:T(8,128)(2,1)S(1)} custom-call(bf16[32,4096]{1,0:T(8,128)(2,1)S(1)} %bitcast.5, bf16[32,4096]{1,0:T(8,128)(2,1)S(1)} %collective-permute-done.1.refs_1_), custom_call_target="tpu_custom_call" | custom-call | flops 1 | bytes 1 | tf_op jit(solution)/shard_map/table/pallas_call | solution.py:135
  8.4 0.8 %product_send.4 = bf16[1024,128]{1,0:T(8,128)(2,1)S(1)} custom-call(s32[1,512]{1,0:T(1,128)S(1)} %get-tuple-element.38.words_ref, bf16[12288,128]{1,0:T(8,128)(2,1)S(1)} %get-tuple-element.36.blocks_ref, bf16[4096,128]{1,0:T(8,128)(2,1)S(1)} %table.2.refs_0_), custom_call_target="tpu_custom_call" | custom-call | flops 1 | bytes 1 | tf_op jit(solution)/shard_map/product_send/pallas_call | solution.py:192
  9.1 1.0 %collective-permute-done.refs_0_ = bf16[32,4096]{1,0:T(8,128)(2,1)S(1)} collective-permute-done((bf16[32,4096]{1,0:T(8,128)(2,1)}, bf16[32,4096]{1,0:T(8,128)(2,1)S(1)}, u32[]{:S(2)}, u32[]{:S(2)}) %collective-permute-start) | collective-permute-done | bytes 262176 | tf_op jit(solution)/shard_map/ppermute | solution.py:311
  10.2 0.5 %collective-permute-start.3 = (bf16[32,4096]{1,0:T(8,128)(2,1)S(1)}, bf16[32,4096]{1,0:T(8,128)(2,1)S(1)}, u32[]{:S(2)}, u32[]{:S(2)}) collective-permute-start(bf16[32,4096]{1,0:T(8,128)(2,1)S(1)} %collective-permute-done.refs_0_), channel_id=1, source_target_pairs={{0,8},{8,0},{16,24},{24,16},{1,9},{9,1},{17,25},{25,17},{2,10},{10... | collective-permute-start | bytes 786440 | tf_op jit(solution)/shard_map/ppermute | solution.py:311
  10.6 1.4 %collective-permute-start.2 = (bf16[1024,128]{1,0:T(8,128)(2,1)S(1)}, bf16[1024,128]{1,0:T(8,128)(2,1)S(1)}, u32[]{:S(2)}, u32[]{:S(2)}) collective-permute-start(bf16[1024,128]{1,0:T(8,128)(2,1)S(1)} %product_send.4), channel_id=1, source_target_pairs={{0,1},{1,0},{2,3},{3,2},{4,5},{5,4},{6,7},{7,6},{8,9},{9,8},{10,11... | collective-permute-start | bytes 786440 | tf_op jit(solution)/shard_map/ppermute | solution.py:311
  12.1 0.7 %table.3.refs_1_.refs_0_ = bf16[4096,128]{1,0:T(8,128)(2,1)S(1)} custom-call(bf16[32,4096]{1,0:T(8,128)(2,1)S(1)} %collective-permute-done.refs_0_, bf16[32,4096]{1,0:T(8,128)(2,1)S(1)} %collective-permute-done.3.refs_1_), custom_call_target="tpu_custom_call" | custom-call | flops 1 | bytes 1 | tf_op jit(solution)/shard_map/table/pallas_call | solution.py:135
  12.8 0.8 %product_send.7 = bf16[512,256]{1,0:T(8,128)(2,1)S(1)} custom-call(s32[1,512]{1,0:T(1,128)S(1)} %get-tuple-element.38.words_ref, bf16[12288,128]{1,0:T(8,128)(2,1)S(1)} %get-tuple-element.36.blocks_ref, bf16[4096,128]{1,0:T(8,128)(2,1)S(1)} %table.2.refs_0_, bf16[4096,128]{1,0:T(8,128)(2,1)S(1)} %table.3.refs_1_.refs_0_), custom_call_target="tpu_custom_call" | custom-call | flops 1 | bytes 1 | tf_op jit(solution)/shard_map/product_send/pallas_call | solution.py:192
  13.6 1.8 %collective-permute-start.12 = (bf16[512,256]{1,0:T(8,128)(2,1)S(1)}, bf16[512,256]{1,0:T(8,128)(2,1)S(1)}, u32[]{:S(2)}, u32[]{:S(2)}) collective-permute-start(bf16[512,256]{1,0:T(8,128)(2,1)S(1)} %product_send.7), channel_id=1, source_target_pairs={{0,2},{1,3},{2,0},{3,1},{4,6},{5,7},{6,4},{7,5},{8,10},{9,11},{10,... | collective-permute-start | bytes 786440 | tf_op jit(solution)/shard_map/ppermute | solution.py:311
  15.3 0.8 %product_send.6 = bf16[512,256]{1,0:T(8,128)(2,1)S(1)} custom-call(s32[1,512]{1,0:T(1,128)S(1)} %get-tuple-element.38.words_ref, bf16[12288,128]{1,0:T(8,128)(2,1)S(1)} %get-tuple-element.36.blocks_ref, bf16[4096,128]{1,0:T(8,128)(2,1)S(1)} %table.2.refs_0_, bf16[4096,128]{1,0:T(8,128)(2,1)S(1)} %table.3.refs_1_.refs_0_), custom_call_target="tpu_custom_call" | custom-call | flops 1 | bytes 1 | tf_op jit(solution)/shard_map/product_send/pallas_call | solution.py:192
  16.1 2.4 %collective-permute-start.9 = (bf16[512,256]{1,0:T(8,128)(2,1)S(1)}, bf16[512,256]{1,0:T(8,128)(2,1)S(1)}, u32[]{:S(2)}, u32[]{:S(2)}) collective-permute-start(bf16[512,256]{1,0:T(8,128)(2,1)S(1)} %product_send.6), channel_id=1, source_target_pairs={{0,1},{1,0},{2,3},{3,2},{4,5},{5,4},{6,7},{7,6},{8,9},{9,8},{10,11... | collective-permute-start | bytes 786440 | tf_op jit(solution)/shard_map/ppermute | solution.py:311
  18.5 0.7 %product_send.5 = bf16[1024,128]{1,0:T(8,128)(2,1)S(1)} custom-call(s32[1,512]{1,0:T(1,128)S(1)} %get-tuple-element.38.words_ref, bf16[12288,128]{1,0:T(8,128)(2,1)S(1)} %get-tuple-element.36.blocks_ref, bf16[4096,128]{1,0:T(8,128)(2,1)S(1)} %table.3.refs_1_.refs_0_), custom_call_target="tpu_custom_call" | custom-call | flops 1 | bytes 1 | tf_op jit(solution)/shard_map/product_send/pallas_call | solution.py:192
  19.2 1.4 %collective-permute-start.6 = (bf16[1024,128]{1,0:T(8,128)(2,1)S(1)}, bf16[1024,128]{1,0:T(8,128)(2,1)S(1)}, u32[]{:S(2)}, u32[]{:S(2)}) collective-permute-start(bf16[1024,128]{1,0:T(8,128)(2,1)S(1)} %product_send.5), channel_id=1, source_target_pairs={{0,1},{1,0},{2,3},{3,2},{4,5},{5,4},{6,7},{7,6},{8,9},{9,8},{10,11... | collective-permute-start | bytes 786440 | tf_op jit(solution)/shard_map/ppermute | solution.py:311
  20.6 1.1 %product_keep.1.keep_ref = f32[2080,256]{1,0:T(8,128)S(1)} custom-call(s32[1,512]{1,0:T(1,128)S(1)} %get-tuple-element.38.words_ref, bf16[12288,128]{1,0:T(8,128)(2,1)S(1)} %get-tuple-element.36.blocks_ref, bf16[4096,128]{1,0:T(8,128)(2,1)S(1)} %table.2.refs_0_, bf16[4096,128]{1,0:T(8,128)(2,1)S(1)} %table.3.refs_1_.refs_0_), custom_call_target="tpu_custom_call" | custom-call | flops 1 | bytes 1 | tf_op jit(solution)/shard_map/product_keep/pallas_call | solution.py:192
  21.7 1.1 %collective-permute-done.12.got_ref = bf16[512,256]{1,0:T(8,128)(2,1)S(1)} collective-permute-done((bf16[512,256]{1,0:T(8,128)(2,1)S(1)}, bf16[512,256]{1,0:T(8,128)(2,1)S(1)}, u32[]{:S(2)}, u32[]{:S(2)}) %collective-permute-start.12) | collective-permute-done | bytes 262176 | tf_op jit(solution)/shard_map/ppermute | solution.py:311
  22.9 5.1 %collective-permute-start.13 = (bf16[256,256]{1,0:T(8,128)(2,1)S(1)}, bf16[256,256]{1,0:T(8,128)(2,1)S(1)}, u32[]{:S(2)}, u32[]{:S(2)}) collective-permute-start(bf16[256,256]{1,0:T(8,128)(2,1)S(1)} %get-tuple-element.54), channel_id=1, source_target_pairs={{0,4},{1,5},{2,6},{3,7},{4,0},{5,1},{6,2},{7,3},{8,12},{9,13},{10,... | collective-permute-start | bytes 393224 | tf_op jit(solution)/shard_map/ppermute | solution.py:311
  28.2 2.1 %collective-permute-start.4 = (bf16[512,128]{1,0:T(8,128)(2,1)S(1)}, bf16[512,128]{1,0:T(8,128)(2,1)S(1)}, u32[]{:S(2)}, u32[]{:S(2)}) collective-permute-start(bf16[512,128]{1,0:T(8,128)(2,1)S(1)} %get-tuple-element.42), channel_id=1, source_target_pairs={{0,2},{1,3},{2,0},{3,1},{4,6},{5,7},{6,4},{7,5},{8,10},{9,11},{10,... | collective-permute-start | bytes 393224 | tf_op jit(solution)/shard_map/ppermute | solution.py:311
  30.3 0.7 %collective-permute-done.6.got_ref = bf16[1024,128]{1,0:T(8,128)(2,1)S(1)} collective-permute-done((bf16[1024,128]{1,0:T(8,128)(2,1)S(1)}, bf16[1024,128]{1,0:T(8,128)(2,1)S(1)}, u32[]{:S(2)}, u32[]{:S(2)}) %collective-permute-start.6) | collective-permute-done | bytes 262176 | tf_op jit(solution)/shard_map/ppermute | solution.py:311
  31.0 1.0 %collective-permute-start.7 = (bf16[512,128]{1,0:T(8,128)(2,1)S(1)}, bf16[512,128]{1,0:T(8,128)(2,1)S(1)}, u32[]{:S(2)}, u32[]{:S(2)}) collective-permute-start(bf16[512,128]{1,0:T(8,128)(2,1)S(1)} %get-tuple-element.46), channel_id=1, source_target_pairs={{0,2},{1,3},{2,0},{3,1},{4,6},{5,7},{6,4},{7,5},{8,10},{9,11},{10,... | collective-permute-start | bytes 393224 | tf_op jit(solution)/shard_map/ppermute | solution.py:311
  32.4 1.3 %collective-permute-start.14 = (bf16[128,256]{1,0:T(8,128)(2,1)S(1)}, bf16[128,256]{1,0:T(8,128)(2,1)S(1)}, u32[]{:S(2)}, u32[]{:S(2)}) collective-permute-start(bf16[128,256]{1,0:T(8,128)(2,1)S(1)} %get-tuple-element.56), channel_id=1, source_target_pairs={{0,1},{1,0},{2,3},{3,2},{4,5},{5,4},{6,7},{7,6},{8,9},{9,8},{10,11... | collective-permute-start | bytes 196616 | tf_op jit(solution)/shard_map/ppermute | solution.py:311
  33.6 1.6 %collective-permute-done.10.got_ref = bf16[256,256]{1,0:T(8,128)(2,1)S(1)} collective-permute-done((bf16[256,256]{1,0:T(8,128)(2,1)S(1)}, bf16[256,256]{1,0:T(8,128)(2,1)S(1)}, u32[]{:S(2)}, u32[]{:S(2)}) %collective-permute-start.10) | collective-permute-done | bytes 131104 | tf_op jit(solution)/shard_map/ppermute | solution.py:311
  35.2 1.1 %collective-permute-start.11 = (bf16[128,256]{1,0:T(8,128)(2,1)S(1)}, bf16[128,256]{1,0:T(8,128)(2,1)S(1)}, u32[]{:S(2)}, u32[]{:S(2)}) collective-permute-start(bf16[128,256]{1,0:T(8,128)(2,1)S(1)} %get-tuple-element.52), channel_id=1, source_target_pairs={{0,4},{1,5},{2,6},{3,7},{4,0},{5,1},{6,2},{7,3},{8,12},{9,13},{10,... | collective-permute-start | bytes 196616 | tf_op jit(solution)/shard_map/ppermute | solution.py:311
  36.3 2.0 %collective-permute-done.4.got_ref = bf16[512,128]{1,0:T(8,128)(2,1)S(1)} collective-permute-done((bf16[512,128]{1,0:T(8,128)(2,1)S(1)}, bf16[512,128]{1,0:T(8,128)(2,1)S(1)}, u32[]{:S(2)}, u32[]{:S(2)}) %collective-permute-start.4) | collective-permute-done | bytes 131104 | tf_op jit(solution)/shard_map/ppermute | solution.py:311
  38.4 1.7 %collective-permute-done.7.got_ref = bf16[512,128]{1,0:T(8,128)(2,1)S(1)} collective-permute-done((bf16[512,128]{1,0:T(8,128)(2,1)S(1)}, bf16[512,128]{1,0:T(8,128)(2,1)S(1)}, u32[]{:S(2)}, u32[]{:S(2)}) %collective-permute-start.7) | collective-permute-done | bytes 131104 | tf_op jit(solution)/shard_map/ppermute | solution.py:311
  40.1 1.3 %collective-permute-start.8 = (bf16[256,128]{1,0:T(8,128)(2,1)S(1)}, bf16[256,128]{1,0:T(8,128)(2,1)S(1)}, u32[]{:S(2)}, u32[]{:S(2)}) collective-permute-start(bf16[256,128]{1,0:T(8,128)(2,1)S(1)} %get-tuple-element.48), channel_id=1, source_target_pairs={{0,4},{1,5},{2,6},{3,7},{4,0},{5,1},{6,2},{7,3},{8,12},{9,13},{10,... | collective-permute-start | bytes 196616 | tf_op jit(solution)/shard_map/ppermute | solution.py:311
  41.4 2.0 %collective-permute-done.11.refs_1_ = bf16[128,256]{1,0:T(8,128)(2,1)S(1)} collective-permute-done((bf16[128,256]{1,0:T(8,128)(2,1)S(1)}, bf16[128,256]{1,0:T(8,128)(2,1)S(1)}, u32[]{:S(2)}, u32[]{:S(2)}) %collective-permute-start.11) | collective-permute-done | bytes 65568 | tf_op jit(solution)/shard_map/ppermute | solution.py:311
  43.4 1.0 %layer_first.1 = (bf16[1024,256]{1,0:T(8,128)(2,1)}, bf16[256,256]{1,0:T(8,128)(2,1)S(1)}, bf16[256,256]{1,0:T(8,128)(2,1)S(1)}) custom-call(f32[128,256]{1,0:T(8,128)S(1)} %get-tuple-element.51.refs_0_, bf16[128,256]{1,0:T(8,128)(2,1)S(1)} %collective-permute-done.11.refs_1_, f32[128,256]{1,0:T(8,128)S(1)} %get-tuple-element.55.refs_2_, ...), custom_call_target="tpu_custom_call" | custom-call | tf_op jit(solution)/shard_map/layer_first/pallas_call | solution.py:288
  44.4 0.7 %collective-permute-done.5.refs_1_ = bf16[256,128]{1,0:T(8,128)(2,1)S(1)} collective-permute-done((bf16[256,128]{1,0:T(8,128)(2,1)S(1)}, bf16[256,128]{1,0:T(8,128)(2,1)S(1)}, u32[]{:S(2)}, u32[]{:S(2)}) %collective-permute-start.5) | collective-permute-done | bytes 65568 | tf_op jit(solution)/shard_map/ppermute | solution.py:311
  45.1 0.7 %collective-permute-done.8.refs_3_ = bf16[256,128]{1,0:T(8,128)(2,1)S(1)} collective-permute-done((bf16[256,128]{1,0:T(8,128)(2,1)S(1)}, bf16[256,128]{1,0:T(8,128)(2,1)S(1)}, u32[]{:S(2)}, u32[]{:S(2)}) %collective-permute-start.8) | collective-permute-done | bytes 65568 | tf_op jit(solution)/shard_map/ppermute | solution.py:311
  45.8 1.0 %layer_last.1 = bf16[1024,256]{1,0:T(8,128)(2,1)} custom-call(f32[256,128]{1,0:T(8,128)S(1)} %get-tuple-element.58.refs_0_, bf16[256,128]{1,0:T(8,128)(2,1)S(1)} %collective-permute-done.5.refs_1_, f32[256,128]{1,0:T(8,128)S(1)} %get-tuple-element.60.refs_2_, bf16[256,128]{1,0:T(8,128)(2,1)S(1)} %collective-permute-done.8.refs_3_, ...), custom_call_target="tpu_custom_call", output_to_operand_aliasing={{}: (7, {})} | custom-call | tf_op jit(solution)/shard_map/layer_last/pallas_call | solution.py:298
  (24 shorter events, 1.2 us)
Async XLA Ops:
  0.0 7.6 %copy-start = (bf16[4096,32]{0,1:T(8,128)(2,1)S(1)}, bf16[4096,32]{0,1:T(8,128)(2,1)}, u32[]{:S(2)}) copy-start(bf16[4096,32]{0,1:T(8,128)(2,1)} %param.6) | copy-start | bytes 786436
  0.0 7.6 %collective-permute-start.1 = (bf16[32,4096]{1,0:T(8,128)(2,1)}, bf16[32,4096]{1,0:T(8,128)(2,1)S(1)}, u32[]{:S(2)}, u32[]{:S(2)}) collective-permute-start(bf16[32,4096]{1,0:T(8,128)(2,1)} %bitcast.3), channel_id=1, source_target_pairs={{0,8},{8,0},{16,24},{24,16},{1,9},{9,1},{17,25},{25,17},{2,10},{10... | collective-permute-start | bytes 786440 | tf_op jit(solution)/shard_map/ppermute | solution.py:311
  0.5 9.7 %collective-permute-start = (bf16[32,4096]{1,0:T(8,128)(2,1)}, bf16[32,4096]{1,0:T(8,128)(2,1)S(1)}, u32[]{:S(2)}, u32[]{:S(2)}) collective-permute-start(bf16[32,4096]{1,0:T(8,128)(2,1)} %bitcast.4), channel_id=1, source_target_pairs={{0,16},{8,24},{16,0},{24,8},{1,17},{9,25},{17,1},{25,9},{2,18},{10... | collective-permute-start | bytes 786440 | tf_op jit(solution)/shard_map/ppermute | solution.py:311
  3.7 0.7 %copy-start.3 = (s32[1,384]{1,0:T(1,128)S(1)}, s32[1,384]{1,0:T(1,128)}, u32[]{:S(2)}) copy-start(s32[1,384]{1,0:T(1,128)} %codes_hbm.1) | copy-start | bytes 4612
  10.2 1.9 %collective-permute-start.3 = (bf16[32,4096]{1,0:T(8,128)(2,1)S(1)}, bf16[32,4096]{1,0:T(8,128)(2,1)S(1)}, u32[]{:S(2)}, u32[]{:S(2)}) collective-permute-start(bf16[32,4096]{1,0:T(8,128)(2,1)S(1)} %collective-permute-done.refs_0_), channel_id=1, source_target_pairs={{0,8},{8,0},{16,24},{24,16},{1,9},{9,1},{17,25},{25,17},{2,10},{10... | collective-permute-start | bytes 786440 | tf_op jit(solution)/shard_map/ppermute | solution.py:311
  10.6 9.9 %collective-permute-start.2 = (bf16[1024,128]{1,0:T(8,128)(2,1)S(1)}, bf16[1024,128]{1,0:T(8,128)(2,1)S(1)}, u32[]{:S(2)}, u32[]{:S(2)}) collective-permute-start(bf16[1024,128]{1,0:T(8,128)(2,1)S(1)} %product_send.4), channel_id=1, source_target_pairs={{0,1},{1,0},{2,3},{3,2},{4,5},{5,4},{6,7},{7,6},{8,9},{9,8},{10,11... | collective-permute-start | bytes 786440 | tf_op jit(solution)/shard_map/ppermute | solution.py:311
  13.6 9.2 %collective-permute-start.12 = (bf16[512,256]{1,0:T(8,128)(2,1)S(1)}, bf16[512,256]{1,0:T(8,128)(2,1)S(1)}, u32[]{:S(2)}, u32[]{:S(2)}) collective-permute-start(bf16[512,256]{1,0:T(8,128)(2,1)S(1)} %product_send.7), channel_id=1, source_target_pairs={{0,2},{1,3},{2,0},{3,1},{4,6},{5,7},{6,4},{7,5},{8,10},{9,11},{10,... | collective-permute-start | bytes 786440 | tf_op jit(solution)/shard_map/ppermute | solution.py:311
  16.1 11.9 %collective-permute-start.9 = (bf16[512,256]{1,0:T(8,128)(2,1)S(1)}, bf16[512,256]{1,0:T(8,128)(2,1)S(1)}, u32[]{:S(2)}, u32[]{:S(2)}) collective-permute-start(bf16[512,256]{1,0:T(8,128)(2,1)S(1)} %product_send.6), channel_id=1, source_target_pairs={{0,1},{1,0},{2,3},{3,2},{4,5},{5,4},{6,7},{7,6},{8,9},{9,8},{10,11... | collective-permute-start | bytes 786440 | tf_op jit(solution)/shard_map/ppermute | solution.py:311
  19.2 11.8 %collective-permute-start.6 = (bf16[1024,128]{1,0:T(8,128)(2,1)S(1)}, bf16[1024,128]{1,0:T(8,128)(2,1)S(1)}, u32[]{:S(2)}, u32[]{:S(2)}) collective-permute-start(bf16[1024,128]{1,0:T(8,128)(2,1)S(1)} %product_send.5), channel_id=1, source_target_pairs={{0,1},{1,0},{2,3},{3,2},{4,5},{5,4},{6,7},{7,6},{8,9},{9,8},{10,11... | collective-permute-start | bytes 786440 | tf_op jit(solution)/shard_map/ppermute | solution.py:311
  22.9 9.5 %collective-permute-start.13 = (bf16[256,256]{1,0:T(8,128)(2,1)S(1)}, bf16[256,256]{1,0:T(8,128)(2,1)S(1)}, u32[]{:S(2)}, u32[]{:S(2)}) collective-permute-start(bf16[256,256]{1,0:T(8,128)(2,1)S(1)} %get-tuple-element.54), channel_id=1, source_target_pairs={{0,4},{1,5},{2,6},{3,7},{4,0},{5,1},{6,2},{7,3},{8,12},{9,13},{10,... | collective-permute-start | bytes 393224 | tf_op jit(solution)/shard_map/ppermute | solution.py:311
  28.0 15.3 %copy-start.1 = (bf16[128,256]{1,0:T(8,128)(2,1)S(1)}, bf16[128,256]{1,0:T(8,128)(2,1)}, u32[]{:S(2)}) copy-start(bf16[128,256]{1,0:T(8,128)(2,1)} %refs_4_.1) | copy-start | bytes 196612
  28.0 15.3 %copy-start.2 = (f32[256]{0:T(256)S(1)}, f32[256]{0:T(256)}, u32[]{:S(2)}) copy-start(f32[256]{0:T(256)} %param.11) | copy-start | bytes 3076
  28.0 7.1 %collective-permute-start.10 = (bf16[256,256]{1,0:T(8,128)(2,1)S(1)}, bf16[256,256]{1,0:T(8,128)(2,1)S(1)}, u32[]{:S(2)}, u32[]{:S(2)}) collective-permute-start(bf16[256,256]{1,0:T(8,128)(2,1)S(1)} %get-tuple-element.50), channel_id=1, source_target_pairs={{0,2},{1,3},{2,0},{3,1},{4,6},{5,7},{6,4},{7,5},{8,10},{9,11},{10,... | collective-permute-start | bytes 393224 | tf_op jit(solution)/shard_map/ppermute | solution.py:311
  28.2 10.1 %collective-permute-start.4 = (bf16[512,128]{1,0:T(8,128)(2,1)S(1)}, bf16[512,128]{1,0:T(8,128)(2,1)S(1)}, u32[]{:S(2)}, u32[]{:S(2)}) collective-permute-start(bf16[512,128]{1,0:T(8,128)(2,1)S(1)} %get-tuple-element.42), channel_id=1, source_target_pairs={{0,2},{1,3},{2,0},{3,1},{4,6},{5,7},{6,4},{7,5},{8,10},{9,11},{10,... | collective-permute-start | bytes 393224 | tf_op jit(solution)/shard_map/ppermute | solution.py:311
  31.0 9.0 %collective-permute-start.7 = (bf16[512,128]{1,0:T(8,128)(2,1)S(1)}, bf16[512,128]{1,0:T(8,128)(2,1)S(1)}, u32[]{:S(2)}, u32[]{:S(2)}) collective-permute-start(bf16[512,128]{1,0:T(8,128)(2,1)S(1)} %get-tuple-element.46), channel_id=1, source_target_pairs={{0,2},{1,3},{2,0},{3,1},{4,6},{5,7},{6,4},{7,5},{8,10},{9,11},{10,... | collective-permute-start | bytes 393224 | tf_op jit(solution)/shard_map/ppermute | solution.py:311
  32.4 9.0 %collective-permute-start.14 = (bf16[128,256]{1,0:T(8,128)(2,1)S(1)}, bf16[128,256]{1,0:T(8,128)(2,1)S(1)}, u32[]{:S(2)}, u32[]{:S(2)}) collective-permute-start(bf16[128,256]{1,0:T(8,128)(2,1)S(1)} %get-tuple-element.56), channel_id=1, source_target_pairs={{0,1},{1,0},{2,3},{3,2},{4,5},{5,4},{6,7},{7,6},{8,9},{9,8},{10,11... | collective-permute-start | bytes 196616 | tf_op jit(solution)/shard_map/ppermute | solution.py:311
  35.2 8.1 %collective-permute-start.11 = (bf16[128,256]{1,0:T(8,128)(2,1)S(1)}, bf16[128,256]{1,0:T(8,128)(2,1)S(1)}, u32[]{:S(2)}, u32[]{:S(2)}) collective-permute-start(bf16[128,256]{1,0:T(8,128)(2,1)S(1)} %get-tuple-element.52), channel_id=1, source_target_pairs={{0,4},{1,5},{2,6},{3,7},{4,0},{5,1},{6,2},{7,3},{8,12},{9,13},{10,... | collective-permute-start | bytes 196616 | tf_op jit(solution)/shard_map/ppermute | solution.py:311
  38.3 6.8 %collective-permute-start.5 = (bf16[256,128]{1,0:T(8,128)(2,1)S(1)}, bf16[256,128]{1,0:T(8,128)(2,1)S(1)}, u32[]{:S(2)}, u32[]{:S(2)}) collective-permute-start(bf16[256,128]{1,0:T(8,128)(2,1)S(1)} %get-tuple-element.44), channel_id=1, source_target_pairs={{0,4},{1,5},{2,6},{3,7},{4,0},{5,1},{6,2},{7,3},{8,12},{9,13},{10,... | collective-permute-start | bytes 196616 | tf_op jit(solution)/shard_map/ppermute | solution.py:311
  40.1 5.7 %collective-permute-start.8 = (bf16[256,128]{1,0:T(8,128)(2,1)S(1)}, bf16[256,128]{1,0:T(8,128)(2,1)S(1)}, u32[]{:S(2)}, u32[]{:S(2)}) collective-permute-start(bf16[256,128]{1,0:T(8,128)(2,1)S(1)} %get-tuple-element.48), channel_id=1, source_target_pairs={{0,4},{1,5},{2,6},{3,7},{4,0},{5,1},{6,2},{7,3},{8,12},{9,13},{10,... | collective-permute-start | bytes 196616 | tf_op jit(solution)/shard_map/ppermute | solution.py:311

commit v2 on v0

--- a/solution.py
+++ b/solution.py
@@ -292,11 +292,13 @@
     other, first = lax.optimization_barrier((other, first))
     far, far_index = spread([other], [1 << top])
     tables.append(make_table(far))
-    sends = [(first, product(0, words, blocks, tables[1:], halves[0], True))]
-    sends += [(product(k, words, blocks, tables, halves[k], True),) for k in (1, 2)]
-    gots = [[exchange(s, "col", n_col, order[0]) for s in send] for send, (_, order) in zip(sends, chunks)]
-    words, gots[0][0] = lax.optimization_barrier((words, gots[0][0]))
+    others = [product(k, words, blocks, tables, halves[k], True) for k in (1, 2)]
+    send = lambda x, k: exchange(x, "col", n_col, chunks[k][1][0])
+    gots = [[send(first, 0)]] + [[send(x, k)] for k, x in enumerate(others, 1)]
+    words, gots[0][0], _ = lax.optimization_barrier((words, gots[0][0], others))
     kept = product(len(chunks), words, blocks, tables, sum(halves), False)
+    words, _ = lax.optimization_barrier((words, kept))
+    gots[0].append(send(product(0, words, blocks, tables[1:], halves[0], True), 0))
     kept_at = [sum(halves[:k]) // halves[k] for k in range(len(chunks))]
     parts = [[(kept, (at, f), got) for f, got in enumerate(g)] for at, g in zip(kept_at, gots)]
     for k in range(1, len(col_axis_bits)):

time: 47.3 us -> 49 us (1.036)
  starting transfers between devices: 23 us -> 18.7 us
  waiting for transfers between devices: 12.3 us -> 16.2 us
  Pallas kernels: 10.6 us -> 12.7 us
    ppermute x15, starting transfers between devices: 23 us -> 18.7 us  [exchange(): return lax.ppermute(x, axis, [(i, i ^ 1 << bit) for i in range(size)])]
    ppermute x15, waiting for transfers between devices: 12.3 us -> 16.2 us  [exchange(): return lax.ppermute(x, axis, [(i, i ^ 1 << bit) for i in range(size)])]
    pallas_call x5, Pallas kernels: 4.39 us -> 6.46 us  [product(): pl.pallas_call(functools.partial(product_kernel, trash, group, len(tables...]
  transfers between devices with their start and end apart: 15 -> 15, of which waited for: 7 -> 9; matrix products, arithmetic and copies ran while one was open for 0% -> 0% of each run, Pallas kernels for 20% -> 23%
where the time goes in v2:
time: 49 us; the launch traced here: 49.1 us
  starting transfers between devices  18.7 us (38%)
  waiting for transfers between devices  16.2 us (33%)
  Pallas kernels  12.7 us (26%)
  between operations  0.84 us (2%)
  local copies, waits for them, and re-layouts  0.69 us (1%)
    ppermute x15, starting transfers between devices, exchange(): return lax.ppermute(x, axis, [(i, i ^ 1 << bit) for i in range(size)])  18.7 us
    ppermute x15, waiting for transfers between devices, exchange(): return lax.ppermute(x, axis, [(i, i ^ 1 << bit) for i in range(size)])  16.2 us
    pallas_call x5, Pallas kernels, product(): pl.pallas_call(functools.partial(product_kernel, trash, group, len(tables...  6.46 us
    pallas_call x1, Pallas kernels, relayout(): pl.pallas_call(functools.partial(relayout_kernel, chunks, col_bits), in_s...  3.24 us
    pallas_call x2, Pallas kernels, make_table(): pl.pallas_call(table_kernel, in_specs=[VMEM] * len(parts), out_specs=VMEM...  1.49 us
    pallas_call x1, Pallas kernels, layer(): pl.pallas_call(functools.partial(layer_kernel, index, [len(part) for part...  1.18 us
  transfers between devices with their start and end apart: 15, of which 9 were waited for; matrix products, arithmetic and copies ran while one was open for 0% of the time, Pallas kernels for 23%

profile of v2, /device:TPU:0, one launch (start us, length us, event | category | flops | bytes accessed | tf_op | source)
XLA Modules:
  0.0 49.1 jit_solution(2779837274904560315)
XLA Ops:
  0.0 0.5 collective-permute-start.1
  0.5 2.6 %collective-permute-start = (bf16[32,4096]{1,0:T(8,128)(2,1)}, bf16[32,4096]{1,0:T(8,128)(2,1)S(1)}, u32[]{:S(2)}, u32[]{:S(2)}) collective-permute-start(bf16[32,4096]{1,0:T(8,128)(2,1)} %bitcast.4), channel_id=1, source_target_pairs={{0,16},{8,24},{16,0},{24,8},{1,17},{9,25},{17,1},{25,9},{2,18},{10... | collective-permute-start | bytes 786440 | tf_op jit(solution)/shard_map/ppermute | solution.py:266
  3.7 0.7 %copy-done.2 = s32[1,384]{1,0:T(1,128)S(1)} copy-done((s32[1,384]{1,0:T(1,128)S(1)}, s32[1,384]{1,0:T(1,128)}, u32[]{:S(2)}) %copy-start.2) | copy-done | bytes 1560
  4.4 3.2 %relayout.1 = (bf16[12288,128]{1,0:T(8,128)(2,1)S(1)}, s32[1,512]{1,0:T(1,128)S(1)}) custom-call(s32[1,1]{1,0:T(1,128)S(6)} %copy.7.count_ref, s32[1,384]{1,0:T(1,128)S(1)} %copy-done.2, bf16[384,4096]{1,0:T(8,128)(2,1)} %bitcast.7), custom_call_target="tpu_custom_call" | custom-call | bytes 6291456 | tf_op jit(solution)/shard_map/relayout/pallas_call | solution.py:99
  7.6 0.7 %table.2.refs_0_ = bf16[4096,128]{1,0:T(8,128)(2,1)S(1)} custom-call(bf16[32,4096]{1,0:T(8,128)(2,1)S(1)} %bitcast.5, bf16[32,4096]{1,0:T(8,128)(2,1)S(1)} %collective-permute-done.1.refs_1_), custom_call_target="tpu_custom_call" | custom-call | flops 1 | bytes 1 | tf_op jit(solution)/shard_map/table/pallas_call | solution.py:135
  8.4 1.2 %product_send.4 = bf16[1024,128]{1,0:T(8,128)(2,1)S(1)} custom-call(s32[1,512]{1,0:T(1,128)S(1)} %get-tuple-element.38.words_ref, bf16[12288,128]{1,0:T(8,128)(2,1)S(1)} %get-tuple-element.29.blocks_ref, bf16[4096,128]{1,0:T(8,128)(2,1)S(1)} %table.2.refs_0_), custom_call_target="tpu_custom_call" | custom-call | flops 1 | bytes 1 | tf_op jit(solution)/shard_map/product_send/pallas_call | solution.py:192
  9.6 0.5 %collective-permute-done.refs_0_ = bf16[32,4096]{1,0:T(8,128)(2,1)S(1)} collective-permute-done((bf16[32,4096]{1,0:T(8,128)(2,1)}, bf16[32,4096]{1,0:T(8,128)(2,1)S(1)}, u32[]{:S(2)}, u32[]{:S(2)}) %collective-permute-start) | collective-permute-done | bytes 262176 | tf_op jit(solution)/shard_map/ppermute | solution.py:266
  10.2 2.2 %collective-permute-start.2 = (bf16[1024,128]{1,0:T(8,128)(2,1)S(1)}, bf16[1024,128]{1,0:T(8,128)(2,1)S(1)}, u32[]{:S(2)}, u32[]{:S(2)}) collective-permute-start(bf16[1024,128]{1,0:T(8,128)(2,1)S(1)} %product_send.4), channel_id=1, source_target_pairs={{0,1},{1,0},{2,3},{3,2},{4,5},{5,4},{6,7},{7,6},{8,9},{9,8},{10,11... | collective-permute-start | bytes 786440 | tf_op jit(solution)/shard_map/ppermute | solution.py:266
  12.3 0.7 %table.3.refs_1_.refs_0_ = bf16[4096,128]{1,0:T(8,128)(2,1)S(1)} custom-call(bf16[32,4096]{1,0:T(8,128)(2,1)S(1)} %collective-permute-done.refs_0_, bf16[32,4096]{1,0:T(8,128)(2,1)S(1)} %collective-permute-done.3.refs_1_), custom_call_target="tpu_custom_call" | custom-call | flops 1 | bytes 1 | tf_op jit(solution)/shard_map/table/pallas_call | solution.py:135
  13.1 1.3 %product_send.6 = bf16[512,256]{1,0:T(8,128)(2,1)S(1)} custom-call(s32[1,512]{1,0:T(1,128)S(1)} %get-tuple-element.38.words_ref, bf16[12288,128]{1,0:T(8,128)(2,1)S(1)} %get-tuple-element.29.blocks_ref, bf16[4096,128]{1,0:T(8,128)(2,1)S(1)} %table.2.refs_0_, bf16[4096,128]{1,0:T(8,128)(2,1)S(1)} %table.3.refs_1_.refs_0_), custom_call_target="tpu_custom_call" | custom-call | flops 1 | bytes 1 | tf_op jit(solution)/shard_map/product_send/pallas_call | solution.py:192
  14.4 1.0 %product_send.5 = bf16[512,256]{1,0:T(8,128)(2,1)S(1)} custom-call(s32[1,512]{1,0:T(1,128)S(1)} %get-tuple-element.38.words_ref, bf16[12288,128]{1,0:T(8,128)(2,1)S(1)} %get-tuple-element.29.blocks_ref, bf16[4096,128]{1,0:T(8,128)(2,1)S(1)} %table.2.refs_0_, bf16[4096,128]{1,0:T(8,128)(2,1)S(1)} %table.3.refs_1_.refs_0_), custom_call_target="tpu_custom_call" | custom-call | flops 1 | bytes 1 | tf_op jit(solution)/shard_map/product_send/pallas_call | solution.py:192
  15.4 2.3 %collective-permute-start.9 = (bf16[512,256]{1,0:T(8,128)(2,1)S(1)}, bf16[512,256]{1,0:T(8,128)(2,1)S(1)}, u32[]{:S(2)}, u32[]{:S(2)}) collective-permute-start(bf16[512,256]{1,0:T(8,128)(2,1)S(1)} %product_send.5), channel_id=1, source_target_pairs={{0,1},{1,0},{2,3},{3,2},{4,5},{5,4},{6,7},{7,6},{8,9},{9,8},{10,11... | collective-permute-start | bytes 786440 | tf_op jit(solution)/shard_map/ppermute | solution.py:266
  17.8 0.8 %collective-permute-start.12 = (bf16[512,256]{1,0:T(8,128)(2,1)S(1)}, bf16[512,256]{1,0:T(8,128)(2,1)S(1)}, u32[]{:S(2)}, u32[]{:S(2)}) collective-permute-start(bf16[512,256]{1,0:T(8,128)(2,1)S(1)} %product_send.6), channel_id=1, source_target_pairs={{0,2},{1,3},{2,0},{3,1},{4,6},{5,7},{6,4},{7,5},{8,10},{9,11},{10,... | collective-permute-start | bytes 786440 | tf_op jit(solution)/shard_map/ppermute | solution.py:266
  18.6 0.9 %collective-permute-done.2.got_ref = bf16[1024,128]{1,0:T(8,128)(2,1)S(1)} collective-permute-done((bf16[1024,128]{1,0:T(8,128)(2,1)S(1)}, bf16[1024,128]{1,0:T(8,128)(2,1)S(1)}, u32[]{:S(2)}, u32[]{:S(2)}) %collective-permute-start.2) | collective-permute-done | bytes 262176 | tf_op jit(solution)/shard_map/ppermute | solution.py:266
  19.5 1.7 %product_keep.1.keep_ref = f32[2080,256]{1,0:T(8,128)S(1)} custom-call(s32[1,512]{1,0:T(1,128)S(1)} %get-tuple-element.38.words_ref, bf16[12288,128]{1,0:T(8,128)(2,1)S(1)} %get-tuple-element.29.blocks_ref, bf16[4096,128]{1,0:T(8,128)(2,1)S(1)} %table.2.refs_0_, bf16[4096,128]{1,0:T(8,128)(2,1)S(1)} %table.3.refs_1_.refs_0_), custom_call_target="tpu_custom_call" | custom-call | flops 1 | bytes 1 | tf_op jit(solution)/shard_map/product_keep/pallas_call | solution.py:192
  21.1 1.2 %product_send.7 = bf16[1024,128]{1,0:T(8,128)(2,1)S(1)} custom-call(s32[1,512]{1,0:T(1,128)S(1)} %get-tuple-element.38.words_ref, bf16[12288,128]{1,0:T(8,128)(2,1)S(1)} %get-tuple-element.29.blocks_ref, bf16[4096,128]{1,0:T(8,128)(2,1)S(1)} %table.3.refs_1_.refs_0_), custom_call_target="tpu_custom_call" | custom-call | flops 1 | bytes 1 | tf_op jit(solution)/shard_map/product_send/pallas_call | solution.py:192
  22.4 5.3 %collective-permute-start.6 = (bf16[1024,128]{1,0:T(8,128)(2,1)S(1)}, bf16[1024,128]{1,0:T(8,128)(2,1)S(1)}, u32[]{:S(2)}, u32[]{:S(2)}) collective-permute-start(bf16[1024,128]{1,0:T(8,128)(2,1)S(1)} %product_send.7), channel_id=1, source_target_pairs={{0,1},{1,0},{2,3},{3,2},{4,5},{5,4},{6,7},{7,6},{8,9},{9,8},{10,11... | collective-permute-start | bytes 786440 | tf_op jit(solution)/shard_map/ppermute | solution.py:266
  27.7 0.1 collective-permute-start.4
  27.9 2.1 %collective-permute-start.10 = (bf16[256,256]{1,0:T(8,128)(2,1)S(1)}, bf16[256,256]{1,0:T(8,128)(2,1)S(1)}, u32[]{:S(2)}, u32[]{:S(2)}) collective-permute-start(bf16[256,256]{1,0:T(8,128)(2,1)S(1)} %get-tuple-element.44), channel_id=1, source_target_pairs={{0,2},{1,3},{2,0},{3,1},{4,6},{5,7},{6,4},{7,5},{8,10},{9,11},{10,... | collective-permute-start | bytes 393224 | tf_op jit(solution)/shard_map/ppermute | solution.py:266
  30.0 0.1 collective-permute-start.13
  30.1 1.9 %collective-permute-done.6.got_ref = bf16[1024,128]{1,0:T(8,128)(2,1)S(1)} collective-permute-done((bf16[1024,128]{1,0:T(8,128)(2,1)S(1)}, bf16[1024,128]{1,0:T(8,128)(2,1)S(1)}, u32[]{:S(2)}, u32[]{:S(2)}) %collective-permute-start.6) | collective-permute-done | bytes 262176 | tf_op jit(solution)/shard_map/ppermute | solution.py:266
  32.1 2.0 %collective-permute-start.7 = (bf16[512,128]{1,0:T(8,128)(2,1)S(1)}, bf16[512,128]{1,0:T(8,128)(2,1)S(1)}, u32[]{:S(2)}, u32[]{:S(2)}) collective-permute-start(bf16[512,128]{1,0:T(8,128)(2,1)S(1)} %get-tuple-element.40), channel_id=1, source_target_pairs={{0,2},{1,3},{2,0},{3,1},{4,6},{5,7},{6,4},{7,5},{8,10},{9,11},{10,... | collective-permute-start | bytes 393224 | tf_op jit(solution)/shard_map/ppermute | solution.py:266
  34.1 1.0 %collective-permute-done.4.got_ref = bf16[512,128]{1,0:T(8,128)(2,1)S(1)} collective-permute-done((bf16[512,128]{1,0:T(8,128)(2,1)S(1)}, bf16[512,128]{1,0:T(8,128)(2,1)S(1)}, u32[]{:S(2)}, u32[]{:S(2)}) %collective-permute-start.4) | collective-permute-done | bytes 131104 | tf_op jit(solution)/shard_map/ppermute | solution.py:266
  35.1 0.1 collective-permute-start.5
  35.2 4.3 %collective-permute-done.10.got_ref = bf16[256,256]{1,0:T(8,128)(2,1)S(1)} collective-permute-done((bf16[256,256]{1,0:T(8,128)(2,1)S(1)}, bf16[256,256]{1,0:T(8,128)(2,1)S(1)}, u32[]{:S(2)}, u32[]{:S(2)}) %collective-permute-start.10) | collective-permute-done | bytes 131104 | tf_op jit(solution)/shard_map/ppermute | solution.py:266
  39.7 0.1 collective-permute-start.14
  39.7 2.4 %collective-permute-done.7.got_ref = bf16[512,128]{1,0:T(8,128)(2,1)S(1)} collective-permute-done((bf16[512,128]{1,0:T(8,128)(2,1)S(1)}, bf16[512,128]{1,0:T(8,128)(2,1)S(1)}, u32[]{:S(2)}, u32[]{:S(2)}) %collective-permute-start.7) | collective-permute-done | bytes 131104 | tf_op jit(solution)/shard_map/ppermute | solution.py:266
  42.2 0.6 %collective-permute-start.8 = (bf16[256,128]{1,0:T(8,128)(2,1)S(1)}, bf16[256,128]{1,0:T(8,128)(2,1)S(1)}, u32[]{:S(2)}, u32[]{:S(2)}) collective-permute-start(bf16[256,128]{1,0:T(8,128)(2,1)S(1)} %get-tuple-element.42), channel_id=1, source_target_pairs={{0,4},{1,5},{2,6},{3,7},{4,0},{5,1},{6,2},{7,3},{8,12},{9,13},{10,... | collective-permute-start | bytes 196616 | tf_op jit(solution)/shard_map/ppermute | solution.py:266
  42.8 1.1 %collective-permute-done.5.refs_1_ = bf16[256,128]{1,0:T(8,128)(2,1)S(1)} collective-permute-done((bf16[256,128]{1,0:T(8,128)(2,1)S(1)}, bf16[256,128]{1,0:T(8,128)(2,1)S(1)}, u32[]{:S(2)}, u32[]{:S(2)}) %collective-permute-start.5) | collective-permute-done | bytes 65568 | tf_op jit(solution)/shard_map/ppermute | solution.py:266
  43.9 2.2 %collective-permute-done.11.refs_5_ = bf16[128,256]{1,0:T(8,128)(2,1)S(1)} collective-permute-done((bf16[128,256]{1,0:T(8,128)(2,1)S(1)}, bf16[128,256]{1,0:T(8,128)(2,1)S(1)}, u32[]{:S(2)}, u32[]{:S(2)}) %collective-permute-start.11) | collective-permute-done | bytes 65568 | tf_op jit(solution)/shard_map/ppermute | solution.py:266
  46.1 1.8 %collective-permute-done.8.refs_3_ = bf16[256,128]{1,0:T(8,128)(2,1)S(1)} collective-permute-done((bf16[256,128]{1,0:T(8,128)(2,1)S(1)}, bf16[256,128]{1,0:T(8,128)(2,1)S(1)}, u32[]{:S(2)}, u32[]{:S(2)}) %collective-permute-start.8) | collective-permute-done | bytes 65568 | tf_op jit(solution)/shard_map/ppermute | solution.py:266
  47.9 1.2 %layer.1 = bf16[1024,256]{1,0:T(8,128)(2,1)} custom-call(f32[256,128]{1,0:T(8,128)S(1)} %get-tuple-element.36.refs_0_, bf16[256,128]{1,0:T(8,128)(2,1)S(1)} %collective-permute-done.5.refs_1_, f32[256,128]{1,0:T(8,128)S(1)} %get-tuple-element.41.refs_2_, bf16[256,128]{1,0:T(8,128)(2,1)S(1)} %collective-permute-done.8.refs_3_, ...), custom_call_target="tpu_custom_call" | custom-call | tf_op jit(solution)/shard_map/layer/pallas_call | solution.py:256
  (23 shorter events, 0.4 us)
Async XLA Ops:
  0.0 7.6 %copy-start = (bf16[4096,32]{0,1:T(8,128)(2,1)S(1)}, bf16[4096,32]{0,1:T(8,128)(2,1)}, u32[]{:S(2)}) copy-start(bf16[4096,32]{0,1:T(8,128)(2,1)} %param.6) | copy-start | bytes 786436
  0.0 7.6 %collective-permute-start.1 = (bf16[32,4096]{1,0:T(8,128)(2,1)}, bf16[32,4096]{1,0:T(8,128)(2,1)S(1)}, u32[]{:S(2)}, u32[]{:S(2)}) collective-permute-start(bf16[32,4096]{1,0:T(8,128)(2,1)} %bitcast.3), channel_id=1, source_target_pairs={{0,8},{8,0},{16,24},{24,16},{1,9},{9,1},{17,25},{25,17},{2,10},{10... | collective-permute-start | bytes 786440 | tf_op jit(solution)/shard_map/ppermute | solution.py:266
  0.5 9.7 %collective-permute-start = (bf16[32,4096]{1,0:T(8,128)(2,1)}, bf16[32,4096]{1,0:T(8,128)(2,1)S(1)}, u32[]{:S(2)}, u32[]{:S(2)}) collective-permute-start(bf16[32,4096]{1,0:T(8,128)(2,1)} %bitcast.4), channel_id=1, source_target_pairs={{0,16},{8,24},{16,0},{24,8},{1,17},{9,25},{17,1},{25,9},{2,18},{10... | collective-permute-start | bytes 786440 | tf_op jit(solution)/shard_map/ppermute | solution.py:266
  3.7 0.7 %copy-start.2 = (s32[1,384]{1,0:T(1,128)S(1)}, s32[1,384]{1,0:T(1,128)}, u32[]{:S(2)}) copy-start(s32[1,384]{1,0:T(1,128)} %codes_hbm.1) | copy-start | bytes 4612
  10.2 2.2 %collective-permute-start.3 = (bf16[32,4096]{1,0:T(8,128)(2,1)S(1)}, bf16[32,4096]{1,0:T(8,128)(2,1)S(1)}, u32[]{:S(2)}, u32[]{:S(2)}) collective-permute-start(bf16[32,4096]{1,0:T(8,128)(2,1)S(1)} %collective-permute-done.refs_0_), channel_id=1, source_target_pairs={{0,8},{8,0},{16,24},{24,16},{1,9},{9,1},{17,25},{25,17},{2,10},{10... | collective-permute-start | bytes 786440 | tf_op jit(solution)/shard_map/ppermute | solution.py:266
  10.2 9.3 %collective-permute-start.2 = (bf16[1024,128]{1,0:T(8,128)(2,1)S(1)}, bf16[1024,128]{1,0:T(8,128)(2,1)S(1)}, u32[]{:S(2)}, u32[]{:S(2)}) collective-permute-start(bf16[1024,128]{1,0:T(8,128)(2,1)S(1)} %product_send.4), channel_id=1, source_target_pairs={{0,1},{1,0},{2,3},{3,2},{4,5},{5,4},{6,7},{7,6},{8,9},{9,8},{10,11... | collective-permute-start | bytes 786440 | tf_op jit(solution)/shard_map/ppermute | solution.py:266
  15.4 12.4 %collective-permute-start.9 = (bf16[512,256]{1,0:T(8,128)(2,1)S(1)}, bf16[512,256]{1,0:T(8,128)(2,1)S(1)}, u32[]{:S(2)}, u32[]{:S(2)}) collective-permute-start(bf16[512,256]{1,0:T(8,128)(2,1)S(1)} %product_send.5), channel_id=1, source_target_pairs={{0,1},{1,0},{2,3},{3,2},{4,5},{5,4},{6,7},{7,6},{8,9},{9,8},{10,11... | collective-permute-start | bytes 786440 | tf_op jit(solution)/shard_map/ppermute | solution.py:266
  17.8 12.2 %collective-permute-start.12 = (bf16[512,256]{1,0:T(8,128)(2,1)S(1)}, bf16[512,256]{1,0:T(8,128)(2,1)S(1)}, u32[]{:S(2)}, u32[]{:S(2)}) collective-permute-start(bf16[512,256]{1,0:T(8,128)(2,1)S(1)} %product_send.6), channel_id=1, source_target_pairs={{0,2},{1,3},{2,0},{3,1},{4,6},{5,7},{6,4},{7,5},{8,10},{9,11},{10,... | collective-permute-start | bytes 786440 | tf_op jit(solution)/shard_map/ppermute | solution.py:266
  22.4 9.6 %collective-permute-start.6 = (bf16[1024,128]{1,0:T(8,128)(2,1)S(1)}, bf16[1024,128]{1,0:T(8,128)(2,1)S(1)}, u32[]{:S(2)}, u32[]{:S(2)}) collective-permute-start(bf16[1024,128]{1,0:T(8,128)(2,1)S(1)} %product_send.7), channel_id=1, source_target_pairs={{0,1},{1,0},{2,3},{3,2},{4,5},{5,4},{6,7},{7,6},{8,9},{9,8},{10,11... | collective-permute-start | bytes 786440 | tf_op jit(solution)/shard_map/ppermute | solution.py:266
  27.7 7.4 %collective-permute-start.4 = (bf16[512,128]{1,0:T(8,128)(2,1)S(1)}, bf16[512,128]{1,0:T(8,128)(2,1)S(1)}, u32[]{:S(2)}, u32[]{:S(2)}) collective-permute-start(bf16[512,128]{1,0:T(8,128)(2,1)S(1)} %get-tuple-element.35), channel_id=1, source_target_pairs={{0,2},{1,3},{2,0},{3,1},{4,6},{5,7},{6,4},{7,5},{8,10},{9,11},{10,... | collective-permute-start | bytes 393224 | tf_op jit(solution)/shard_map/ppermute | solution.py:266
  27.9 20.1 %copy-start.1 = (bf16[128,256]{1,0:T(8,128)(2,1)S(1)}, bf16[128,256]{1,0:T(8,128)(2,1)}, u32[]{:S(2)}) copy-start(bf16[128,256]{1,0:T(8,128)(2,1)} %refs_8_.1) | copy-start | bytes 196612
  27.9 20.1 %copy-start.3 = (f32[256]{0:T(256)S(1)}, f32[256]{0:T(256)}, u32[]{:S(2)}) copy-start(f32[256]{0:T(256)} %param.11) | copy-start | bytes 3076
  27.9 11.6 %collective-permute-start.10 = (bf16[256,256]{1,0:T(8,128)(2,1)S(1)}, bf16[256,256]{1,0:T(8,128)(2,1)S(1)}, u32[]{:S(2)}, u32[]{:S(2)}) collective-permute-start(bf16[256,256]{1,0:T(8,128)(2,1)S(1)} %get-tuple-element.44), channel_id=1, source_target_pairs={{0,2},{1,3},{2,0},{3,1},{4,6},{5,7},{6,4},{7,5},{8,10},{9,11},{10,... | collective-permute-start | bytes 393224 | tf_op jit(solution)/shard_map/ppermute | solution.py:266
  30.0 9.6 %collective-permute-start.13 = (bf16[256,256]{1,0:T(8,128)(2,1)S(1)}, bf16[256,256]{1,0:T(8,128)(2,1)S(1)}, u32[]{:S(2)}, u32[]{:S(2)}) collective-permute-start(bf16[256,256]{1,0:T(8,128)(2,1)S(1)} %get-tuple-element.48), channel_id=1, source_target_pairs={{0,4},{1,5},{2,6},{3,7},{4,0},{5,1},{6,2},{7,3},{8,12},{9,13},{10,... | collective-permute-start | bytes 393224 | tf_op jit(solution)/shard_map/ppermute | solution.py:266
  32.1 10.1 %collective-permute-start.7 = (bf16[512,128]{1,0:T(8,128)(2,1)S(1)}, bf16[512,128]{1,0:T(8,128)(2,1)S(1)}, u32[]{:S(2)}, u32[]{:S(2)}) collective-permute-start(bf16[512,128]{1,0:T(8,128)(2,1)S(1)} %get-tuple-element.40), channel_id=1, source_target_pairs={{0,2},{1,3},{2,0},{3,1},{4,6},{5,7},{6,4},{7,5},{8,10},{9,11},{10,... | collective-permute-start | bytes 393224 | tf_op jit(solution)/shard_map/ppermute | solution.py:266
  35.1 8.7 %collective-permute-start.5 = (bf16[256,128]{1,0:T(8,128)(2,1)S(1)}, bf16[256,128]{1,0:T(8,128)(2,1)S(1)}, u32[]{:S(2)}, u32[]{:S(2)}) collective-permute-start(bf16[256,128]{1,0:T(8,128)(2,1)S(1)} %get-tuple-element.37), channel_id=1, source_target_pairs={{0,4},{1,5},{2,6},{3,7},{4,0},{5,1},{6,2},{7,3},{8,12},{9,13},{10,... | collective-permute-start | bytes 196616 | tf_op jit(solution)/shard_map/ppermute | solution.py:266
  39.5 6.5 %collective-permute-start.11 = (bf16[128,256]{1,0:T(8,128)(2,1)S(1)}, bf16[128,256]{1,0:T(8,128)(2,1)S(1)}, u32[]{:S(2)}, u32[]{:S(2)}) collective-permute-start(bf16[128,256]{1,0:T(8,128)(2,1)S(1)} %get-tuple-element.46), channel_id=1, source_target_pairs={{0,4},{1,5},{2,6},{3,7},{4,0},{5,1},{6,2},{7,3},{8,12},{9,13},{10,... | collective-permute-start | bytes 196616 | tf_op jit(solution)/shard_map/ppermute | solution.py:266
  39.7 6.4 %collective-permute-start.14 = (bf16[128,256]{1,0:T(8,128)(2,1)S(1)}, bf16[128,256]{1,0:T(8,128)(2,1)S(1)}, u32[]{:S(2)}, u32[]{:S(2)}) collective-permute-start(bf16[128,256]{1,0:T(8,128)(2,1)S(1)} %get-tuple-element.50), channel_id=1, source_target_pairs={{0,1},{1,0},{2,3},{3,2},{4,5},{5,4},{6,7},{7,6},{8,9},{9,8},{10,11... | collective-permute-start | bytes 196616 | tf_op jit(solution)/shard_map/ppermute | solution.py:266
  42.2 5.8 %collective-permute-start.8 = (bf16[256,128]{1,0:T(8,128)(2,1)S(1)}, bf16[256,128]{1,0:T(8,128)(2,1)S(1)}, u32[]{:S(2)}, u32[]{:S(2)}) collective-permute-start(bf16[256,128]{1,0:T(8,128)(2,1)S(1)} %get-tuple-element.42), channel_id=1, source_target_pairs={{0,4},{1,5},{2,6},{3,7},{4,0},{5,1},{6,2},{7,3},{8,12},{9,13},{10,... | collective-permute-start | bytes 196616 | tf_op jit(solution)/shard_map/ppermute | solution.py:266

commit v3 on v0

--- a/solution.py
+++ b/solution.py
@@ -12,7 +12,7 @@
 LANES = 2 * BLK
 GROUP = 16
 TOGETHER = 4
-UNROLL = 16
+UNROLL = 24
 SLOT_AT, SOURCE_AT = 13, 7
 MIB = 1024 * 1024
 SMEM = pl.BlockSpec(memory_space=pltpu.SMEM)

time: 47.3 us -> 46.3 us (0.979); the launches traced: 47.4 us -> 45.5 us
  waiting for transfers between devices: 12.3 us -> 7.35 us
  Pallas kernels: 10.6 us -> 14.4 us
  starting transfers between devices: 23 us -> 22.3 us
    ppermute x15, waiting for transfers between devices: 12.3 us -> 7.35 us  [exchange(): return lax.ppermute(x, axis, [(i, i ^ 1 << bit) for i in range(size)])]
    pallas_call x5, Pallas kernels: 4.39 us -> 8.18 us  [product(): pl.pallas_call(functools.partial(product_kernel, trash, group, len(tables...]
    ppermute x15, starting transfers between devices: 23 us -> 22.3 us  [exchange(): return lax.ppermute(x, axis, [(i, i ^ 1 << bit) for i in range(size)])]
  transfers between devices with their start and end apart: 15 -> 15, of which waited for: 7 -> 4; matrix products, arithmetic and copies ran while one was open for 0% -> 0% of each run, Pallas kernels for 20% -> 29%
where the time goes in v3:
time: 46.3 us; the launch traced here: 45.5 us
  starting transfers between devices  22.3 us (48%)
  Pallas kernels  14.4 us (31%)
  waiting for transfers between devices  7.35 us (16%)
  between operations  0.78 us (2%)
  local copies, waits for them, and re-layouts  0.69 us (1%)
    ppermute x15, starting transfers between devices, exchange(): return lax.ppermute(x, axis, [(i, i ^ 1 << bit) for i in range(size)])  22.3 us
    pallas_call x5, Pallas kernels, product(): pl.pallas_call(functools.partial(product_kernel, trash, group, len(tables...  8.18 us
    ppermute x15, waiting for transfers between devices, exchange(): return lax.ppermute(x, axis, [(i, i ^ 1 << bit) for i in range(size)])  7.35 us
    pallas_call x1, Pallas kernels, relayout(): pl.pallas_call(functools.partial(relayout_kernel, chunks, col_bits), in_s...  3.24 us
    pallas_call x2, Pallas kernels, make_table(): pl.pallas_call(table_kernel, in_specs=[VMEM] * len(parts), out_specs=VMEM...  1.49 us
    pallas_call x1, Pallas kernels, layer(): pl.pallas_call(functools.partial(layer_kernel, index, [len(part) for part...  1.18 us
  transfers between devices with their start and end apart: 15, of which 4 were waited for; matrix products, arithmetic and copies ran while one was open for 0% of the time, Pallas kernels for 29%

profile of v3, /device:TPU:0, one launch (start us, length us, event | category | flops | bytes accessed | tf_op | source)
XLA Modules:
  0.0 45.5 jit_solution(7968319365899255057)
XLA Ops:
  0.0 0.5 collective-permute-start.1
  0.5 2.6 %collective-permute-start = (bf16[32,4096]{1,0:T(8,128)(2,1)}, bf16[32,4096]{1,0:T(8,128)(2,1)S(1)}, u32[]{:S(2)}, u32[]{:S(2)}) collective-permute-start(bf16[32,4096]{1,0:T(8,128)(2,1)} %bitcast.4), channel_id=1, source_target_pairs={{0,16},{8,24},{16,0},{24,8},{1,17},{9,25},{17,1},{25,9},{2,18},{10... | collective-permute-start | bytes 786440 | tf_op jit(solution)/shard_map/ppermute | solution.py:266
  3.7 0.7 %copy-done.2 = s32[1,384]{1,0:T(1,128)S(1)} copy-done((s32[1,384]{1,0:T(1,128)S(1)}, s32[1,384]{1,0:T(1,128)}, u32[]{:S(2)}) %copy-start.2) | copy-done | bytes 1560
  4.4 3.2 %relayout.1 = (bf16[12288,128]{1,0:T(8,128)(2,1)S(1)}, s32[1,512]{1,0:T(1,128)S(1)}) custom-call(s32[1,1]{1,0:T(1,128)S(6)} %copy.7.count_ref, s32[1,384]{1,0:T(1,128)S(1)} %copy-done.2, bf16[384,4096]{1,0:T(8,128)(2,1)} %bitcast.7), custom_call_target="tpu_custom_call" | custom-call | bytes 6291456 | tf_op jit(solution)/shard_map/relayout/pallas_call | solution.py:99
  7.6 0.0 collective-permute-done.1.refs_1_
  7.6 0.7 %table.2.refs_0_ = bf16[4096,128]{1,0:T(8,128)(2,1)S(1)} custom-call(bf16[32,4096]{1,0:T(8,128)(2,1)S(1)} %bitcast.5, bf16[32,4096]{1,0:T(8,128)(2,1)S(1)} %collective-permute-done.1.refs_1_), custom_call_target="tpu_custom_call" | custom-call | flops 1 | bytes 1 | tf_op jit(solution)/shard_map/table/pallas_call | solution.py:135
  8.4 1.4 %product_send.4 = bf16[1024,128]{1,0:T(8,128)(2,1)S(1)} custom-call(s32[1,512]{1,0:T(1,128)S(1)} %get-tuple-element.30.words_ref, bf16[12288,128]{1,0:T(8,128)(2,1)S(1)} %get-tuple-element.28.blocks_ref, bf16[4096,128]{1,0:T(8,128)(2,1)S(1)} %table.2.refs_0_), custom_call_target="tpu_custom_call" | custom-call | flops 1 | bytes 1 | tf_op jit(solution)/shard_map/product_send/pallas_call | solution.py:192
  9.8 0.3 collective-permute-done.refs_0_
  10.2 1.7 %collective-permute-start.2 = (bf16[1024,128]{1,0:T(8,128)(2,1)S(1)}, bf16[1024,128]{1,0:T(8,128)(2,1)S(1)}, u32[]{:S(2)}, u32[]{:S(2)}) collective-permute-start(bf16[1024,128]{1,0:T(8,128)(2,1)S(1)} %product_send.4), channel_id=1, source_target_pairs={{0,1},{1,0},{2,3},{3,2},{4,5},{5,4},{6,7},{7,6},{8,9},{9,8},{10,11... | collective-permute-start | bytes 786440 | tf_op jit(solution)/shard_map/ppermute | solution.py:266
  11.9 0.7 %table.3.refs_1_.refs_0_ = bf16[4096,128]{1,0:T(8,128)(2,1)S(1)} custom-call(bf16[32,4096]{1,0:T(8,128)(2,1)S(1)} %collective-permute-done.refs_0_, bf16[32,4096]{1,0:T(8,128)(2,1)S(1)} %collective-permute-done.3.refs_1_), custom_call_target="tpu_custom_call" | custom-call | flops 1 | bytes 1 | tf_op jit(solution)/shard_map/table/pallas_call | solution.py:135
  12.6 1.5 %product_send.7 = bf16[512,256]{1,0:T(8,128)(2,1)S(1)} custom-call(s32[1,512]{1,0:T(1,128)S(1)} %get-tuple-element.30.words_ref, bf16[12288,128]{1,0:T(8,128)(2,1)S(1)} %get-tuple-element.28.blocks_ref, bf16[4096,128]{1,0:T(8,128)(2,1)S(1)} %table.2.refs_0_, bf16[4096,128]{1,0:T(8,128)(2,1)S(1)} %table.3.refs_1_.refs_0_), custom_call_target="tpu_custom_call" | custom-call | flops 1 | bytes 1 | tf_op jit(solution)/shard_map/product_send/pallas_call | solution.py:192
  14.2 2.0 %collective-permute-start.12 = (bf16[512,256]{1,0:T(8,128)(2,1)S(1)}, bf16[512,256]{1,0:T(8,128)(2,1)S(1)}, u32[]{:S(2)}, u32[]{:S(2)}) collective-permute-start(bf16[512,256]{1,0:T(8,128)(2,1)S(1)} %product_send.7), channel_id=1, source_target_pairs={{0,2},{1,3},{2,0},{3,1},{4,6},{5,7},{6,4},{7,5},{8,10},{9,11},{10,... | collective-permute-start | bytes 786440 | tf_op jit(solution)/shard_map/ppermute | solution.py:266
  16.1 1.1 %product_send.6 = bf16[512,256]{1,0:T(8,128)(2,1)S(1)} custom-call(s32[1,512]{1,0:T(1,128)S(1)} %get-tuple-element.30.words_ref, bf16[12288,128]{1,0:T(8,128)(2,1)S(1)} %get-tuple-element.28.blocks_ref, bf16[4096,128]{1,0:T(8,128)(2,1)S(1)} %table.2.refs_0_, bf16[4096,128]{1,0:T(8,128)(2,1)S(1)} %table.3.refs_1_.refs_0_), custom_call_target="tpu_custom_call" | custom-call | flops 1 | bytes 1 | tf_op jit(solution)/shard_map/product_send/pallas_call | solution.py:192
  17.3 1.6 %collective-permute-start.9 = (bf16[512,256]{1,0:T(8,128)(2,1)S(1)}, bf16[512,256]{1,0:T(8,128)(2,1)S(1)}, u32[]{:S(2)}, u32[]{:S(2)}) collective-permute-start(bf16[512,256]{1,0:T(8,128)(2,1)S(1)} %product_send.6), channel_id=1, source_target_pairs={{0,1},{1,0},{2,3},{3,2},{4,5},{5,4},{6,7},{7,6},{8,9},{9,8},{10,11... | collective-permute-start | bytes 786440 | tf_op jit(solution)/shard_map/ppermute | solution.py:266
  18.9 1.4 %product_send.5 = bf16[1024,128]{1,0:T(8,128)(2,1)S(1)} custom-call(s32[1,512]{1,0:T(1,128)S(1)} %get-tuple-element.30.words_ref, bf16[12288,128]{1,0:T(8,128)(2,1)S(1)} %get-tuple-element.28.blocks_ref, bf16[4096,128]{1,0:T(8,128)(2,1)S(1)} %table.3.refs_1_.refs_0_), custom_call_target="tpu_custom_call" | custom-call | flops 1 | bytes 1 | tf_op jit(solution)/shard_map/product_send/pallas_call | solution.py:192
  20.3 0.9 %collective-permute-start.6 = (bf16[1024,128]{1,0:T(8,128)(2,1)S(1)}, bf16[1024,128]{1,0:T(8,128)(2,1)S(1)}, u32[]{:S(2)}, u32[]{:S(2)}) collective-permute-start(bf16[1024,128]{1,0:T(8,128)(2,1)S(1)} %product_send.5), channel_id=1, source_target_pairs={{0,1},{1,0},{2,3},{3,2},{4,5},{5,4},{6,7},{7,6},{8,9},{9,8},{10,11... | collective-permute-start | bytes 786440 | tf_op jit(solution)/shard_map/ppermute | solution.py:266
  21.2 2.7 %product_keep.1.keep_ref = f32[2080,256]{1,0:T(8,128)S(1)} custom-call(s32[1,512]{1,0:T(1,128)S(1)} %get-tuple-element.30.words_ref, bf16[12288,128]{1,0:T(8,128)(2,1)S(1)} %get-tuple-element.28.blocks_ref, bf16[4096,128]{1,0:T(8,128)(2,1)S(1)} %table.2.refs_0_, bf16[4096,128]{1,0:T(8,128)(2,1)S(1)} %table.3.refs_1_.refs_0_), custom_call_target="tpu_custom_call" | custom-call | flops 1 | bytes 1 | tf_op jit(solution)/shard_map/product_keep/pallas_call | solution.py:192
  23.9 1.3 %collective-permute-start.4 = (bf16[512,128]{1,0:T(8,128)(2,1)S(1)}, bf16[512,128]{1,0:T(8,128)(2,1)S(1)}, u32[]{:S(2)}, u32[]{:S(2)}) collective-permute-start(bf16[512,128]{1,0:T(8,128)(2,1)S(1)} %get-tuple-element.34), channel_id=1, source_target_pairs={{0,2},{1,3},{2,0},{3,1},{4,6},{5,7},{6,4},{7,5},{8,10},{9,11},{10,... | collective-permute-start | bytes 393224 | tf_op jit(solution)/shard_map/ppermute | solution.py:266
  25.2 0.0 copy-start.1
  25.3 0.0 copy-start.3
  25.3 1.7 %collective-permute-start.13 = (bf16[256,256]{1,0:T(8,128)(2,1)S(1)}, bf16[256,256]{1,0:T(8,128)(2,1)S(1)}, u32[]{:S(2)}, u32[]{:S(2)}) collective-permute-start(bf16[256,256]{1,0:T(8,128)(2,1)S(1)} %get-tuple-element.46), channel_id=1, source_target_pairs={{0,4},{1,5},{2,6},{3,7},{4,0},{5,1},{6,2},{7,3},{8,12},{9,13},{10,... | collective-permute-start | bytes 393224 | tf_op jit(solution)/shard_map/ppermute | solution.py:266
  27.0 1.2 %collective-permute-start.10 = (bf16[256,256]{1,0:T(8,128)(2,1)S(1)}, bf16[256,256]{1,0:T(8,128)(2,1)S(1)}, u32[]{:S(2)}, u32[]{:S(2)}) collective-permute-start(bf16[256,256]{1,0:T(8,128)(2,1)S(1)} %get-tuple-element.42), channel_id=1, source_target_pairs={{0,2},{1,3},{2,0},{3,1},{4,6},{5,7},{6,4},{7,5},{8,10},{9,11},{10,... | collective-permute-start | bytes 393224 | tf_op jit(solution)/shard_map/ppermute | solution.py:266
  28.2 2.1 %collective-permute-done.6.got_ref = bf16[1024,128]{1,0:T(8,128)(2,1)S(1)} collective-permute-done((bf16[1024,128]{1,0:T(8,128)(2,1)S(1)}, bf16[1024,128]{1,0:T(8,128)(2,1)S(1)}, u32[]{:S(2)}, u32[]{:S(2)}) %collective-permute-start.6) | collective-permute-done | bytes 262176 | tf_op jit(solution)/shard_map/ppermute | solution.py:266
  30.4 0.1 add.10
  30.4 1.8 %collective-permute-start.7 = (bf16[512,128]{1,0:T(8,128)(2,1)S(1)}, bf16[512,128]{1,0:T(8,128)(2,1)S(1)}, u32[]{:S(2)}, u32[]{:S(2)}) collective-permute-start(bf16[512,128]{1,0:T(8,128)(2,1)S(1)} %get-tuple-element.38), channel_id=1, source_target_pairs={{0,2},{1,3},{2,0},{3,1},{4,6},{5,7},{6,4},{7,5},{8,10},{9,11},{10,... | collective-permute-start | bytes 393224 | tf_op jit(solution)/shard_map/ppermute | solution.py:266
  32.3 2.4 %collective-permute-start.5 = (bf16[256,128]{1,0:T(8,128)(2,1)S(1)}, bf16[256,128]{1,0:T(8,128)(2,1)S(1)}, u32[]{:S(2)}, u32[]{:S(2)}) collective-permute-start(bf16[256,128]{1,0:T(8,128)(2,1)S(1)} %get-tuple-element.36), channel_id=1, source_target_pairs={{0,4},{1,5},{2,6},{3,7},{4,0},{5,1},{6,2},{7,3},{8,12},{9,13},{10,... | collective-permute-start | bytes 196616 | tf_op jit(solution)/shard_map/ppermute | solution.py:266
  34.8 1.6 %collective-permute-start.14 = (bf16[128,256]{1,0:T(8,128)(2,1)S(1)}, bf16[128,256]{1,0:T(8,128)(2,1)S(1)}, u32[]{:S(2)}, u32[]{:S(2)}) collective-permute-start(bf16[128,256]{1,0:T(8,128)(2,1)S(1)} %get-tuple-element.48), channel_id=1, source_target_pairs={{0,1},{1,0},{2,3},{3,2},{4,5},{5,4},{6,7},{7,6},{8,9},{9,8},{10,11... | collective-permute-start | bytes 196616 | tf_op jit(solution)/shard_map/ppermute | solution.py:266
  36.4 1.3 %collective-permute-start.11 = (bf16[128,256]{1,0:T(8,128)(2,1)S(1)}, bf16[128,256]{1,0:T(8,128)(2,1)S(1)}, u32[]{:S(2)}, u32[]{:S(2)}) collective-permute-start(bf16[128,256]{1,0:T(8,128)(2,1)S(1)} %get-tuple-element.44), channel_id=1, source_target_pairs={{0,4},{1,5},{2,6},{3,7},{4,0},{5,1},{6,2},{7,3},{8,12},{9,13},{10,... | collective-permute-start | bytes 196616 | tf_op jit(solution)/shard_map/ppermute | solution.py:266
  37.7 1.8 %collective-permute-start.8 = (bf16[256,128]{1,0:T(8,128)(2,1)S(1)}, bf16[256,128]{1,0:T(8,128)(2,1)S(1)}, u32[]{:S(2)}, u32[]{:S(2)}) collective-permute-start(bf16[256,128]{1,0:T(8,128)(2,1)S(1)} %get-tuple-element.40), channel_id=1, source_target_pairs={{0,4},{1,5},{2,6},{3,7},{4,0},{5,1},{6,2},{7,3},{8,12},{9,13},{10,... | collective-permute-start | bytes 196616 | tf_op jit(solution)/shard_map/ppermute | solution.py:266
  39.5 3.5 %collective-permute-done.11.refs_5_ = bf16[128,256]{1,0:T(8,128)(2,1)S(1)} collective-permute-done((bf16[128,256]{1,0:T(8,128)(2,1)S(1)}, bf16[128,256]{1,0:T(8,128)(2,1)S(1)}, u32[]{:S(2)}, u32[]{:S(2)}) %collective-permute-start.11) | collective-permute-done | bytes 65568 | tf_op jit(solution)/shard_map/ppermute | solution.py:266
  43.0 1.4 %collective-permute-done.8.refs_3_ = bf16[256,128]{1,0:T(8,128)(2,1)S(1)} collective-permute-done((bf16[256,128]{1,0:T(8,128)(2,1)S(1)}, bf16[256,128]{1,0:T(8,128)(2,1)S(1)}, u32[]{:S(2)}, u32[]{:S(2)}) %collective-permute-start.8) | collective-permute-done | bytes 65568 | tf_op jit(solution)/shard_map/ppermute | solution.py:266
  44.4 1.2 %layer.1 = bf16[1024,256]{1,0:T(8,128)(2,1)} custom-call(f32[256,128]{1,0:T(8,128)S(1)} %get-tuple-element.35.refs_0_, bf16[256,128]{1,0:T(8,128)(2,1)S(1)} %collective-permute-done.5.refs_1_, f32[256,128]{1,0:T(8,128)S(1)} %get-tuple-element.39.refs_2_, bf16[256,128]{1,0:T(8,128)(2,1)S(1)} %collective-permute-done.8.refs_3_, ...), custom_call_target="tpu_custom_call" | custom-call | tf_op jit(solution)/shard_map/layer/pallas_call | solution.py:256
  (23 shorter events, 0.3 us)
Async XLA Ops:
  0.0 7.6 %copy-start = (bf16[4096,32]{0,1:T(8,128)(2,1)S(1)}, bf16[4096,32]{0,1:T(8,128)(2,1)}, u32[]{:S(2)}) copy-start(bf16[4096,32]{0,1:T(8,128)(2,1)} %param.6) | copy-start | bytes 786436
  0.0 7.6 %collective-permute-start.1 = (bf16[32,4096]{1,0:T(8,128)(2,1)}, bf16[32,4096]{1,0:T(8,128)(2,1)S(1)}, u32[]{:S(2)}, u32[]{:S(2)}) collective-permute-start(bf16[32,4096]{1,0:T(8,128)(2,1)} %bitcast.3), channel_id=1, source_target_pairs={{0,8},{8,0},{16,24},{24,16},{1,9},{9,1},{17,25},{25,17},{2,10},{10... | collective-permute-start | bytes 786440 | tf_op jit(solution)/shard_map/ppermute | solution.py:266
  0.5 9.7 %collective-permute-start = (bf16[32,4096]{1,0:T(8,128)(2,1)}, bf16[32,4096]{1,0:T(8,128)(2,1)S(1)}, u32[]{:S(2)}, u32[]{:S(2)}) collective-permute-start(bf16[32,4096]{1,0:T(8,128)(2,1)} %bitcast.4), channel_id=1, source_target_pairs={{0,16},{8,24},{16,0},{24,8},{1,17},{9,25},{17,1},{25,9},{2,18},{10... | collective-permute-start | bytes 786440 | tf_op jit(solution)/shard_map/ppermute | solution.py:266
  3.7 0.7 %copy-start.2 = (s32[1,384]{1,0:T(1,128)S(1)}, s32[1,384]{1,0:T(1,128)}, u32[]{:S(2)}) copy-start(s32[1,384]{1,0:T(1,128)} %codes_hbm.1) | copy-start | bytes 4612
  10.2 1.7 %collective-permute-start.3 = (bf16[32,4096]{1,0:T(8,128)(2,1)S(1)}, bf16[32,4096]{1,0:T(8,128)(2,1)S(1)}, u32[]{:S(2)}, u32[]{:S(2)}) collective-permute-start(bf16[32,4096]{1,0:T(8,128)(2,1)S(1)} %collective-permute-done.refs_0_), channel_id=1, source_target_pairs={{0,8},{8,0},{16,24},{24,16},{1,9},{9,1},{17,25},{25,17},{2,10},{10... | collective-permute-start | bytes 786440 | tf_op jit(solution)/shard_map/ppermute | solution.py:266
  10.2 11.0 %collective-permute-start.2 = (bf16[1024,128]{1,0:T(8,128)(2,1)S(1)}, bf16[1024,128]{1,0:T(8,128)(2,1)S(1)}, u32[]{:S(2)}, u32[]{:S(2)}) collective-permute-start(bf16[1024,128]{1,0:T(8,128)(2,1)S(1)} %product_send.4), channel_id=1, source_target_pairs={{0,1},{1,0},{2,3},{3,2},{4,5},{5,4},{6,7},{7,6},{8,9},{9,8},{10,11... | collective-permute-start | bytes 786440 | tf_op jit(solution)/shard_map/ppermute | solution.py:266
  14.2 11.0 %collective-permute-start.12 = (bf16[512,256]{1,0:T(8,128)(2,1)S(1)}, bf16[512,256]{1,0:T(8,128)(2,1)S(1)}, u32[]{:S(2)}, u32[]{:S(2)}) collective-permute-start(bf16[512,256]{1,0:T(8,128)(2,1)S(1)} %product_send.7), channel_id=1, source_target_pairs={{0,2},{1,3},{2,0},{3,1},{4,6},{5,7},{6,4},{7,5},{8,10},{9,11},{10,... | collective-permute-start | bytes 786440 | tf_op jit(solution)/shard_map/ppermute | solution.py:266
  17.3 9.7 %collective-permute-start.9 = (bf16[512,256]{1,0:T(8,128)(2,1)S(1)}, bf16[512,256]{1,0:T(8,128)(2,1)S(1)}, u32[]{:S(2)}, u32[]{:S(2)}) collective-permute-start(bf16[512,256]{1,0:T(8,128)(2,1)S(1)} %product_send.6), channel_id=1, source_target_pairs={{0,1},{1,0},{2,3},{3,2},{4,5},{5,4},{6,7},{7,6},{8,9},{9,8},{10,11... | collective-permute-start | bytes 786440 | tf_op jit(solution)/shard_map/ppermute | solution.py:266
  20.3 10.0 %collective-permute-start.6 = (bf16[1024,128]{1,0:T(8,128)(2,1)S(1)}, bf16[1024,128]{1,0:T(8,128)(2,1)S(1)}, u32[]{:S(2)}, u32[]{:S(2)}) collective-permute-start(bf16[1024,128]{1,0:T(8,128)(2,1)S(1)} %product_send.5), channel_id=1, source_target_pairs={{0,1},{1,0},{2,3},{3,2},{4,5},{5,4},{6,7},{7,6},{8,9},{9,8},{10,11... | collective-permute-start | bytes 786440 | tf_op jit(solution)/shard_map/ppermute | solution.py:266
  23.9 8.4 %collective-permute-start.4 = (bf16[512,128]{1,0:T(8,128)(2,1)S(1)}, bf16[512,128]{1,0:T(8,128)(2,1)S(1)}, u32[]{:S(2)}, u32[]{:S(2)}) collective-permute-start(bf16[512,128]{1,0:T(8,128)(2,1)S(1)} %get-tuple-element.34), channel_id=1, source_target_pairs={{0,2},{1,3},{2,0},{3,1},{4,6},{5,7},{6,4},{7,5},{8,10},{9,11},{10,... | collective-permute-start | bytes 393224 | tf_op jit(solution)/shard_map/ppermute | solution.py:266
  25.2 19.1 %copy-start.1 = (bf16[128,256]{1,0:T(8,128)(2,1)S(1)}, bf16[128,256]{1,0:T(8,128)(2,1)}, u32[]{:S(2)}) copy-start(bf16[128,256]{1,0:T(8,128)(2,1)} %refs_8_.1) | copy-start | bytes 196612
  25.3 19.1 %copy-start.3 = (f32[256]{0:T(256)S(1)}, f32[256]{0:T(256)}, u32[]{:S(2)}) copy-start(f32[256]{0:T(256)} %param.11) | copy-start | bytes 3076
  25.3 9.5 %collective-permute-start.13 = (bf16[256,256]{1,0:T(8,128)(2,1)S(1)}, bf16[256,256]{1,0:T(8,128)(2,1)S(1)}, u32[]{:S(2)}, u32[]{:S(2)}) collective-permute-start(bf16[256,256]{1,0:T(8,128)(2,1)S(1)} %get-tuple-element.46), channel_id=1, source_target_pairs={{0,4},{1,5},{2,6},{3,7},{4,0},{5,1},{6,2},{7,3},{8,12},{9,13},{10,... | collective-permute-start | bytes 393224 | tf_op jit(solution)/shard_map/ppermute | solution.py:266
  27.0 9.3 %collective-permute-start.10 = (bf16[256,256]{1,0:T(8,128)(2,1)S(1)}, bf16[256,256]{1,0:T(8,128)(2,1)S(1)}, u32[]{:S(2)}, u32[]{:S(2)}) collective-permute-start(bf16[256,256]{1,0:T(8,128)(2,1)S(1)} %get-tuple-element.42), channel_id=1, source_target_pairs={{0,2},{1,3},{2,0},{3,1},{4,6},{5,7},{6,4},{7,5},{8,10},{9,11},{10,... | collective-permute-start | bytes 393224 | tf_op jit(solution)/shard_map/ppermute | solution.py:266
  30.4 7.2 %collective-permute-start.7 = (bf16[512,128]{1,0:T(8,128)(2,1)S(1)}, bf16[512,128]{1,0:T(8,128)(2,1)S(1)}, u32[]{:S(2)}, u32[]{:S(2)}) collective-permute-start(bf16[512,128]{1,0:T(8,128)(2,1)S(1)} %get-tuple-element.38), channel_id=1, source_target_pairs={{0,2},{1,3},{2,0},{3,1},{4,6},{5,7},{6,4},{7,5},{8,10},{9,11},{10,... | collective-permute-start | bytes 393224 | tf_op jit(solution)/shard_map/ppermute | solution.py:266
  32.3 7.2 %collective-permute-start.5 = (bf16[256,128]{1,0:T(8,128)(2,1)S(1)}, bf16[256,128]{1,0:T(8,128)(2,1)S(1)}, u32[]{:S(2)}, u32[]{:S(2)}) collective-permute-start(bf16[256,128]{1,0:T(8,128)(2,1)S(1)} %get-tuple-element.36), channel_id=1, source_target_pairs={{0,4},{1,5},{2,6},{3,7},{4,0},{5,1},{6,2},{7,3},{8,12},{9,13},{10,... | collective-permute-start | bytes 196616 | tf_op jit(solution)/shard_map/ppermute | solution.py:266
  34.8 4.7 %collective-permute-start.14 = (bf16[128,256]{1,0:T(8,128)(2,1)S(1)}, bf16[128,256]{1,0:T(8,128)(2,1)S(1)}, u32[]{:S(2)}, u32[]{:S(2)}) collective-permute-start(bf16[128,256]{1,0:T(8,128)(2,1)S(1)} %get-tuple-element.48), channel_id=1, source_target_pairs={{0,1},{1,0},{2,3},{3,2},{4,5},{5,4},{6,7},{7,6},{8,9},{9,8},{10,11... | collective-permute-start | bytes 196616 | tf_op jit(solution)/shard_map/ppermute | solution.py:266
  36.4 6.6 %collective-permute-start.11 = (bf16[128,256]{1,0:T(8,128)(2,1)S(1)}, bf16[128,256]{1,0:T(8,128)(2,1)S(1)}, u32[]{:S(2)}, u32[]{:S(2)}) collective-permute-start(bf16[128,256]{1,0:T(8,128)(2,1)S(1)} %get-tuple-element.44), channel_id=1, source_target_pairs={{0,4},{1,5},{2,6},{3,7},{4,0},{5,1},{6,2},{7,3},{8,12},{9,13},{10,... | collective-permute-start | bytes 196616 | tf_op jit(solution)/shard_map/ppermute | solution.py:266
  37.7 6.7 %collective-permute-start.8 = (bf16[256,128]{1,0:T(8,128)(2,1)S(1)}, bf16[256,128]{1,0:T(8,128)(2,1)S(1)}, u32[]{:S(2)}, u32[]{:S(2)}) collective-permute-start(bf16[256,128]{1,0:T(8,128)(2,1)S(1)} %get-tuple-element.40), channel_id=1, source_target_pairs={{0,4},{1,5},{2,6},{3,7},{4,0},{5,1},{6,2},{7,3},{8,12},{9,13},{10,... | collective-permute-start | bytes 196616 | tf_op jit(solution)/shard_map/ppermute | solution.py:266

commit v4 on v0

--- a/solution.py
+++ b/solution.py
@@ -11,7 +11,7 @@
 PAIR = BLK // 2
 LANES = 2 * BLK
 GROUP = 16
-TOGETHER = 4
+TOGETHER = 2
 UNROLL = 16
 SLOT_AT, SOURCE_AT = 13, 7
 MIB = 1024 * 1024

time: 47.3 us -> 46.1 us (0.975)
  waiting for transfers between devices: 12.3 us -> 9.13 us
  starting transfers between devices: 23 us -> 24.2 us
  Pallas kernels: 10.6 us -> 11.4 us
    ppermute x15, waiting for transfers between devices: 12.3 us -> 9.13 us  [exchange(): return lax.ppermute(x, axis, [(i, i ^ 1 << bit) for i in range(size)])]
    ppermute x15, starting transfers between devices: 23 us -> 24.2 us  [exchange(): return lax.ppermute(x, axis, [(i, i ^ 1 << bit) for i in range(size)])]
    pallas_call x5, Pallas kernels: 4.39 us -> 5.16 us  [product(): pl.pallas_call(functools.partial(product_kernel, trash, group, len(tables...]
  transfers between devices with their start and end apart: 15 -> 15, of which waited for: 7 -> 6; matrix products, arithmetic and copies ran while one was open for 0% -> 0% of each run, Pallas kernels for 20% -> 22%
where the time goes in v4:
time: 46.1 us
  starting transfers between devices  24.2 us (52%)
  Pallas kernels  11.4 us (25%)
  waiting for transfers between devices  9.13 us (20%)
  between operations  0.78 us (2%)
  local copies, waits for them, and re-layouts  0.69 us (1%)
    ppermute x15, starting transfers between devices, exchange(): return lax.ppermute(x, axis, [(i, i ^ 1 << bit) for i in range(size)])  24.2 us
    ppermute x15, waiting for transfers between devices, exchange(): return lax.ppermute(x, axis, [(i, i ^ 1 << bit) for i in range(size)])  9.13 us
    pallas_call x5, Pallas kernels, product(): pl.pallas_call(functools.partial(product_kernel, trash, group, len(tables...  5.16 us
    pallas_call x1, Pallas kernels, relayout(): pl.pallas_call(functools.partial(relayout_kernel, chunks, col_bits), in_s...  3.2 us
    pallas_call x2, Pallas kernels, make_table(): pl.pallas_call(table_kernel, in_specs=[VMEM] * len(parts), out_specs=VMEM...  1.49 us
    pallas_call x1, Pallas kernels, layer(): pl.pallas_call(functools.partial(layer_kernel, index, [len(part) for part...  1.19 us
  transfers between devices with their start and end apart: 15, of which 6 were waited for; matrix products, arithmetic and copies ran while one was open for 0% of the time, Pallas kernels for 22%

profile of v4, /device:TPU:0, one launch (start us, length us, event | category | flops | bytes accessed | tf_op | source)
XLA Modules:
  0.0 46.1 jit_solution(2197606231596915731)
XLA Ops:
  0.0 0.5 collective-permute-start.1
  0.5 2.6 %collective-permute-start = (bf16[32,4096]{1,0:T(8,128)(2,1)}, bf16[32,4096]{1,0:T(8,128)(2,1)S(1)}, u32[]{:S(2)}, u32[]{:S(2)}) collective-permute-start(bf16[32,4096]{1,0:T(8,128)(2,1)} %bitcast.4), channel_id=1, source_target_pairs={{0,16},{8,24},{16,0},{24,8},{1,17},{9,25},{17,1},{25,9},{2,18},{10... | collective-permute-start | bytes 786440 | tf_op jit(solution)/shard_map/ppermute | solution.py:266
  3.7 0.7 %copy-done.2 = s32[1,384]{1,0:T(1,128)S(1)} copy-done((s32[1,384]{1,0:T(1,128)S(1)}, s32[1,384]{1,0:T(1,128)}, u32[]{:S(2)}) %copy-start.2) | copy-done | bytes 1560
  4.4 3.2 %relayout.1 = (bf16[12288,128]{1,0:T(8,128)(2,1)S(1)}, s32[1,512]{1,0:T(1,128)S(1)}) custom-call(s32[1,1]{1,0:T(1,128)S(6)} %copy.7.count_ref, s32[1,384]{1,0:T(1,128)S(1)} %copy-done.2, bf16[384,4096]{1,0:T(8,128)(2,1)} %bitcast.7), custom_call_target="tpu_custom_call" | custom-call | bytes 6291456 | tf_op jit(solution)/shard_map/relayout/pallas_call | solution.py:99
  7.6 0.7 %table.2.refs_0_ = bf16[4096,128]{1,0:T(8,128)(2,1)S(1)} custom-call(bf16[32,4096]{1,0:T(8,128)(2,1)S(1)} %bitcast.5, bf16[32,4096]{1,0:T(8,128)(2,1)S(1)} %collective-permute-done.1.refs_1_), custom_call_target="tpu_custom_call" | custom-call | flops 1 | bytes 1 | tf_op jit(solution)/shard_map/table/pallas_call | solution.py:135
  8.3 1.0 %product_send.4 = bf16[1024,128]{1,0:T(8,128)(2,1)S(1)} custom-call(s32[1,512]{1,0:T(1,128)S(1)} %get-tuple-element.30.words_ref, bf16[12288,128]{1,0:T(8,128)(2,1)S(1)} %get-tuple-element.28.blocks_ref, bf16[4096,128]{1,0:T(8,128)(2,1)S(1)} %table.2.refs_0_), custom_call_target="tpu_custom_call" | custom-call | flops 1 | bytes 1 | tf_op jit(solution)/shard_map/product_send/pallas_call | solution.py:192
  9.4 0.8 %collective-permute-done.refs_0_ = bf16[32,4096]{1,0:T(8,128)(2,1)S(1)} collective-permute-done((bf16[32,4096]{1,0:T(8,128)(2,1)}, bf16[32,4096]{1,0:T(8,128)(2,1)S(1)}, u32[]{:S(2)}, u32[]{:S(2)}) %collective-permute-start) | collective-permute-done | bytes 262176 | tf_op jit(solution)/shard_map/ppermute | solution.py:266
  10.2 0.2 collective-permute-start.3
  10.3 1.5 %collective-permute-start.2 = (bf16[1024,128]{1,0:T(8,128)(2,1)S(1)}, bf16[1024,128]{1,0:T(8,128)(2,1)S(1)}, u32[]{:S(2)}, u32[]{:S(2)}) collective-permute-start(bf16[1024,128]{1,0:T(8,128)(2,1)S(1)} %product_send.4), channel_id=1, source_target_pairs={{0,1},{1,0},{2,3},{3,2},{4,5},{5,4},{6,7},{7,6},{8,9},{9,8},{10,11... | collective-permute-start | bytes 786440 | tf_op jit(solution)/shard_map/ppermute | solution.py:266
  11.9 0.7 %table.3.refs_1_.refs_0_ = bf16[4096,128]{1,0:T(8,128)(2,1)S(1)} custom-call(bf16[32,4096]{1,0:T(8,128)(2,1)S(1)} %collective-permute-done.refs_0_, bf16[32,4096]{1,0:T(8,128)(2,1)S(1)} %collective-permute-done.3.refs_1_), custom_call_target="tpu_custom_call" | custom-call | flops 1 | bytes 1 | tf_op jit(solution)/shard_map/table/pallas_call | solution.py:135
  12.6 1.0 %product_send.7 = bf16[512,256]{1,0:T(8,128)(2,1)S(1)} custom-call(s32[1,512]{1,0:T(1,128)S(1)} %get-tuple-element.30.words_ref, bf16[12288,128]{1,0:T(8,128)(2,1)S(1)} %get-tuple-element.28.blocks_ref, bf16[4096,128]{1,0:T(8,128)(2,1)S(1)} %table.2.refs_0_, bf16[4096,128]{1,0:T(8,128)(2,1)S(1)} %table.3.refs_1_.refs_0_), custom_call_target="tpu_custom_call" | custom-call | flops 1 | bytes 1 | tf_op jit(solution)/shard_map/product_send/pallas_call | solution.py:192
  13.7 1.7 %collective-permute-start.12 = (bf16[512,256]{1,0:T(8,128)(2,1)S(1)}, bf16[512,256]{1,0:T(8,128)(2,1)S(1)}, u32[]{:S(2)}, u32[]{:S(2)}) collective-permute-start(bf16[512,256]{1,0:T(8,128)(2,1)S(1)} %product_send.7), channel_id=1, source_target_pairs={{0,2},{1,3},{2,0},{3,1},{4,6},{5,7},{6,4},{7,5},{8,10},{9,11},{10,... | collective-permute-start | bytes 786440 | tf_op jit(solution)/shard_map/ppermute | solution.py:266
  15.3 1.0 %product_send.6 = bf16[512,256]{1,0:T(8,128)(2,1)S(1)} custom-call(s32[1,512]{1,0:T(1,128)S(1)} %get-tuple-element.30.words_ref, bf16[12288,128]{1,0:T(8,128)(2,1)S(1)} %get-tuple-element.28.blocks_ref, bf16[4096,128]{1,0:T(8,128)(2,1)S(1)} %table.2.refs_0_, bf16[4096,128]{1,0:T(8,128)(2,1)S(1)} %table.3.refs_1_.refs_0_), custom_call_target="tpu_custom_call" | custom-call | flops 1 | bytes 1 | tf_op jit(solution)/shard_map/product_send/pallas_call | solution.py:192
  16.4 2.4 %collective-permute-start.9 = (bf16[512,256]{1,0:T(8,128)(2,1)S(1)}, bf16[512,256]{1,0:T(8,128)(2,1)S(1)}, u32[]{:S(2)}, u32[]{:S(2)}) collective-permute-start(bf16[512,256]{1,0:T(8,128)(2,1)S(1)} %product_send.6), channel_id=1, source_target_pairs={{0,1},{1,0},{2,3},{3,2},{4,5},{5,4},{6,7},{7,6},{8,9},{9,8},{10,11... | collective-permute-start | bytes 786440 | tf_op jit(solution)/shard_map/ppermute | solution.py:266
  18.7 1.0 %product_send.5 = bf16[1024,128]{1,0:T(8,128)(2,1)S(1)} custom-call(s32[1,512]{1,0:T(1,128)S(1)} %get-tuple-element.30.words_ref, bf16[12288,128]{1,0:T(8,128)(2,1)S(1)} %get-tuple-element.28.blocks_ref, bf16[4096,128]{1,0:T(8,128)(2,1)S(1)} %table.3.refs_1_.refs_0_), custom_call_target="tpu_custom_call" | custom-call | flops 1 | bytes 1 | tf_op jit(solution)/shard_map/product_send/pallas_call | solution.py:192
  19.8 0.6 %collective-permute-start.6 = (bf16[1024,128]{1,0:T(8,128)(2,1)S(1)}, bf16[1024,128]{1,0:T(8,128)(2,1)S(1)}, u32[]{:S(2)}, u32[]{:S(2)}) collective-permute-start(bf16[1024,128]{1,0:T(8,128)(2,1)S(1)} %product_send.5), channel_id=1, source_target_pairs={{0,1},{1,0},{2,3},{3,2},{4,5},{5,4},{6,7},{7,6},{8,9},{9,8},{10,11... | collective-permute-start | bytes 786440 | tf_op jit(solution)/shard_map/ppermute | solution.py:266
  20.3 1.1 %product_keep.1.keep_ref = f32[2080,256]{1,0:T(8,128)S(1)} custom-call(s32[1,512]{1,0:T(1,128)S(1)} %get-tuple-element.30.words_ref, bf16[12288,128]{1,0:T(8,128)(2,1)S(1)} %get-tuple-element.28.blocks_ref, bf16[4096,128]{1,0:T(8,128)(2,1)S(1)} %table.2.refs_0_, bf16[4096,128]{1,0:T(8,128)(2,1)S(1)} %table.3.refs_1_.refs_0_), custom_call_target="tpu_custom_call" | custom-call | flops 1 | bytes 1 | tf_op jit(solution)/shard_map/product_keep/pallas_call | solution.py:192
  21.5 0.6 %collective-permute-start.4 = (bf16[512,128]{1,0:T(8,128)(2,1)S(1)}, bf16[512,128]{1,0:T(8,128)(2,1)S(1)}, u32[]{:S(2)}, u32[]{:S(2)}) collective-permute-start(bf16[512,128]{1,0:T(8,128)(2,1)S(1)} %get-tuple-element.34), channel_id=1, source_target_pairs={{0,2},{1,3},{2,0},{3,1},{4,6},{5,7},{6,4},{7,5},{8,10},{9,11},{10,... | collective-permute-start | bytes 393224 | tf_op jit(solution)/shard_map/ppermute | solution.py:266
  22.1 0.5 %collective-permute-done.12.got_ref = bf16[512,256]{1,0:T(8,128)(2,1)S(1)} collective-permute-done((bf16[512,256]{1,0:T(8,128)(2,1)S(1)}, bf16[512,256]{1,0:T(8,128)(2,1)S(1)}, u32[]{:S(2)}, u32[]{:S(2)}) %collective-permute-start.12) | collective-permute-done | bytes 262176 | tf_op jit(solution)/shard_map/ppermute | solution.py:266
  22.7 4.5 %collective-permute-start.13 = (bf16[256,256]{1,0:T(8,128)(2,1)S(1)}, bf16[256,256]{1,0:T(8,128)(2,1)S(1)}, u32[]{:S(2)}, u32[]{:S(2)}) collective-permute-start(bf16[256,256]{1,0:T(8,128)(2,1)S(1)} %get-tuple-element.46), channel_id=1, source_target_pairs={{0,4},{1,5},{2,6},{3,7},{4,0},{5,1},{6,2},{7,3},{8,12},{9,13},{10,... | collective-permute-start | bytes 393224 | tf_op jit(solution)/shard_map/ppermute | solution.py:266
  27.2 2.1 %collective-permute-start.10 = (bf16[256,256]{1,0:T(8,128)(2,1)S(1)}, bf16[256,256]{1,0:T(8,128)(2,1)S(1)}, u32[]{:S(2)}, u32[]{:S(2)}) collective-permute-start(bf16[256,256]{1,0:T(8,128)(2,1)S(1)} %get-tuple-element.42), channel_id=1, source_target_pairs={{0,2},{1,3},{2,0},{3,1},{4,6},{5,7},{6,4},{7,5},{8,10},{9,11},{10,... | collective-permute-start | bytes 393224 | tf_op jit(solution)/shard_map/ppermute | solution.py:266
  29.3 1.8 %collective-permute-done.6.got_ref = bf16[1024,128]{1,0:T(8,128)(2,1)S(1)} collective-permute-done((bf16[1024,128]{1,0:T(8,128)(2,1)S(1)}, bf16[1024,128]{1,0:T(8,128)(2,1)S(1)}, u32[]{:S(2)}, u32[]{:S(2)}) %collective-permute-start.6) | collective-permute-done | bytes 262176 | tf_op jit(solution)/shard_map/ppermute | solution.py:266
  31.1 0.1 add.10
  31.1 0.9 %collective-permute-start.7 = (bf16[512,128]{1,0:T(8,128)(2,1)S(1)}, bf16[512,128]{1,0:T(8,128)(2,1)S(1)}, u32[]{:S(2)}, u32[]{:S(2)}) collective-permute-start(bf16[512,128]{1,0:T(8,128)(2,1)S(1)} %get-tuple-element.38), channel_id=1, source_target_pairs={{0,2},{1,3},{2,0},{3,1},{4,6},{5,7},{6,4},{7,5},{8,10},{9,11},{10,... | collective-permute-start | bytes 393224 | tf_op jit(solution)/shard_map/ppermute | solution.py:266
  32.1 2.7 %collective-permute-start.5 = (bf16[256,128]{1,0:T(8,128)(2,1)S(1)}, bf16[256,128]{1,0:T(8,128)(2,1)S(1)}, u32[]{:S(2)}, u32[]{:S(2)}) collective-permute-start(bf16[256,128]{1,0:T(8,128)(2,1)S(1)} %get-tuple-element.36), channel_id=1, source_target_pairs={{0,4},{1,5},{2,6},{3,7},{4,0},{5,1},{6,2},{7,3},{8,12},{9,13},{10,... | collective-permute-start | bytes 196616 | tf_op jit(solution)/shard_map/ppermute | solution.py:266
  34.8 1.8 %collective-permute-start.14 = (bf16[128,256]{1,0:T(8,128)(2,1)S(1)}, bf16[128,256]{1,0:T(8,128)(2,1)S(1)}, u32[]{:S(2)}, u32[]{:S(2)}) collective-permute-start(bf16[128,256]{1,0:T(8,128)(2,1)S(1)} %get-tuple-element.48), channel_id=1, source_target_pairs={{0,1},{1,0},{2,3},{3,2},{4,5},{5,4},{6,7},{7,6},{8,9},{9,8},{10,11... | collective-permute-start | bytes 196616 | tf_op jit(solution)/shard_map/ppermute | solution.py:266
  36.7 0.1 collective-permute-start.11
  36.8 0.9 %collective-permute-done.7.got_ref = bf16[512,128]{1,0:T(8,128)(2,1)S(1)} collective-permute-done((bf16[512,128]{1,0:T(8,128)(2,1)S(1)}, bf16[512,128]{1,0:T(8,128)(2,1)S(1)}, u32[]{:S(2)}, u32[]{:S(2)}) %collective-permute-start.7) | collective-permute-done | bytes 131104 | tf_op jit(solution)/shard_map/ppermute | solution.py:266
  37.7 2.1 %collective-permute-start.8 = (bf16[256,128]{1,0:T(8,128)(2,1)S(1)}, bf16[256,128]{1,0:T(8,128)(2,1)S(1)}, u32[]{:S(2)}, u32[]{:S(2)}) collective-permute-start(bf16[256,128]{1,0:T(8,128)(2,1)S(1)} %get-tuple-element.40), channel_id=1, source_target_pairs={{0,4},{1,5},{2,6},{3,7},{4,0},{5,1},{6,2},{7,3},{8,12},{9,13},{10,... | collective-permute-start | bytes 196616 | tf_op jit(solution)/shard_map/ppermute | solution.py:266
  39.8 4.4 %collective-permute-done.11.refs_5_ = bf16[128,256]{1,0:T(8,128)(2,1)S(1)} collective-permute-done((bf16[128,256]{1,0:T(8,128)(2,1)S(1)}, bf16[128,256]{1,0:T(8,128)(2,1)S(1)}, u32[]{:S(2)}, u32[]{:S(2)}) %collective-permute-start.11) | collective-permute-done | bytes 65568 | tf_op jit(solution)/shard_map/ppermute | solution.py:266
  44.2 0.7 %collective-permute-done.8.refs_3_ = bf16[256,128]{1,0:T(8,128)(2,1)S(1)} collective-permute-done((bf16[256,128]{1,0:T(8,128)(2,1)S(1)}, bf16[256,128]{1,0:T(8,128)(2,1)S(1)}, u32[]{:S(2)}, u32[]{:S(2)}) %collective-permute-start.8) | collective-permute-done | bytes 65568 | tf_op jit(solution)/shard_map/ppermute | solution.py:266
  44.9 1.2 %layer.1 = bf16[1024,256]{1,0:T(8,128)(2,1)} custom-call(f32[256,128]{1,0:T(8,128)S(1)} %get-tuple-element.35.refs_0_, bf16[256,128]{1,0:T(8,128)(2,1)S(1)} %collective-permute-done.5.refs_1_, f32[256,128]{1,0:T(8,128)S(1)} %get-tuple-element.39.refs_2_, bf16[256,128]{1,0:T(8,128)(2,1)S(1)} %collective-permute-done.8.refs_3_, ...), custom_call_target="tpu_custom_call" | custom-call | tf_op jit(solution)/shard_map/layer/pallas_call | solution.py:256
  (23 shorter events, 0.3 us)
Async XLA Ops:
  0.0 7.6 %copy-start = (bf16[4096,32]{0,1:T(8,128)(2,1)S(1)}, bf16[4096,32]{0,1:T(8,128)(2,1)}, u32[]{:S(2)}) copy-start(bf16[4096,32]{0,1:T(8,128)(2,1)} %param.6) | copy-start | bytes 786436
  0.0 7.6 %collective-permute-start.1 = (bf16[32,4096]{1,0:T(8,128)(2,1)}, bf16[32,4096]{1,0:T(8,128)(2,1)S(1)}, u32[]{:S(2)}, u32[]{:S(2)}) collective-permute-start(bf16[32,4096]{1,0:T(8,128)(2,1)} %bitcast.3), channel_id=1, source_target_pairs={{0,8},{8,0},{16,24},{24,16},{1,9},{9,1},{17,25},{25,17},{2,10},{10... | collective-permute-start | bytes 786440 | tf_op jit(solution)/shard_map/ppermute | solution.py:266
  0.5 9.7 %collective-permute-start = (bf16[32,4096]{1,0:T(8,128)(2,1)}, bf16[32,4096]{1,0:T(8,128)(2,1)S(1)}, u32[]{:S(2)}, u32[]{:S(2)}) collective-permute-start(bf16[32,4096]{1,0:T(8,128)(2,1)} %bitcast.4), channel_id=1, source_target_pairs={{0,16},{8,24},{16,0},{24,8},{1,17},{9,25},{17,1},{25,9},{2,18},{10... | collective-permute-start | bytes 786440 | tf_op jit(solution)/shard_map/ppermute | solution.py:266
  3.7 0.7 %copy-start.2 = (s32[1,384]{1,0:T(1,128)S(1)}, s32[1,384]{1,0:T(1,128)}, u32[]{:S(2)}) copy-start(s32[1,384]{1,0:T(1,128)} %codes_hbm.1) | copy-start | bytes 4612
  10.2 1.7 %collective-permute-start.3 = (bf16[32,4096]{1,0:T(8,128)(2,1)S(1)}, bf16[32,4096]{1,0:T(8,128)(2,1)S(1)}, u32[]{:S(2)}, u32[]{:S(2)}) collective-permute-start(bf16[32,4096]{1,0:T(8,128)(2,1)S(1)} %collective-permute-done.refs_0_), channel_id=1, source_target_pairs={{0,8},{8,0},{16,24},{24,16},{1,9},{9,1},{17,25},{25,17},{2,10},{10... | collective-permute-start | bytes 786440 | tf_op jit(solution)/shard_map/ppermute | solution.py:266
  10.3 10.0 %collective-permute-start.2 = (bf16[1024,128]{1,0:T(8,128)(2,1)S(1)}, bf16[1024,128]{1,0:T(8,128)(2,1)S(1)}, u32[]{:S(2)}, u32[]{:S(2)}) collective-permute-start(bf16[1024,128]{1,0:T(8,128)(2,1)S(1)} %product_send.4), channel_id=1, source_target_pairs={{0,1},{1,0},{2,3},{3,2},{4,5},{5,4},{6,7},{7,6},{8,9},{9,8},{10,11... | collective-permute-start | bytes 786440 | tf_op jit(solution)/shard_map/ppermute | solution.py:266
  13.7 9.0 %collective-permute-start.12 = (bf16[512,256]{1,0:T(8,128)(2,1)S(1)}, bf16[512,256]{1,0:T(8,128)(2,1)S(1)}, u32[]{:S(2)}, u32[]{:S(2)}) collective-permute-start(bf16[512,256]{1,0:T(8,128)(2,1)S(1)} %product_send.7), channel_id=1, source_target_pairs={{0,2},{1,3},{2,0},{3,1},{4,6},{5,7},{6,4},{7,5},{8,10},{9,11},{10,... | collective-permute-start | bytes 786440 | tf_op jit(solution)/shard_map/ppermute | solution.py:266
  16.4 10.8 %collective-permute-start.9 = (bf16[512,256]{1,0:T(8,128)(2,1)S(1)}, bf16[512,256]{1,0:T(8,128)(2,1)S(1)}, u32[]{:S(2)}, u32[]{:S(2)}) collective-permute-start(bf16[512,256]{1,0:T(8,128)(2,1)S(1)} %product_send.6), channel_id=1, source_target_pairs={{0,1},{1,0},{2,3},{3,2},{4,5},{5,4},{6,7},{7,6},{8,9},{9,8},{10,11... | collective-permute-start | bytes 786440 | tf_op jit(solution)/shard_map/ppermute | solution.py:266
  19.8 11.3 %collective-permute-start.6 = (bf16[1024,128]{1,0:T(8,128)(2,1)S(1)}, bf16[1024,128]{1,0:T(8,128)(2,1)S(1)}, u32[]{:S(2)}, u32[]{:S(2)}) collective-permute-start(bf16[1024,128]{1,0:T(8,128)(2,1)S(1)} %product_send.5), channel_id=1, source_target_pairs={{0,1},{1,0},{2,3},{3,2},{4,5},{5,4},{6,7},{7,6},{8,9},{9,8},{10,11... | collective-permute-start | bytes 786440 | tf_op jit(solution)/shard_map/ppermute | solution.py:266
  21.5 10.6 %collective-permute-start.4 = (bf16[512,128]{1,0:T(8,128)(2,1)S(1)}, bf16[512,128]{1,0:T(8,128)(2,1)S(1)}, u32[]{:S(2)}, u32[]{:S(2)}) collective-permute-start(bf16[512,128]{1,0:T(8,128)(2,1)S(1)} %get-tuple-element.34), channel_id=1, source_target_pairs={{0,2},{1,3},{2,0},{3,1},{4,6},{5,7},{6,4},{7,5},{8,10},{9,11},{10,... | collective-permute-start | bytes 393224 | tf_op jit(solution)/shard_map/ppermute | solution.py:266
  22.7 22.3 %copy-start.1 = (bf16[128,256]{1,0:T(8,128)(2,1)S(1)}, bf16[128,256]{1,0:T(8,128)(2,1)}, u32[]{:S(2)}) copy-start(bf16[128,256]{1,0:T(8,128)(2,1)} %refs_8_.1) | copy-start | bytes 196612
  22.7 22.3 %copy-start.3 = (f32[256]{0:T(256)S(1)}, f32[256]{0:T(256)}, u32[]{:S(2)}) copy-start(f32[256]{0:T(256)} %param.11) | copy-start | bytes 3076
  22.7 12.1 %collective-permute-start.13 = (bf16[256,256]{1,0:T(8,128)(2,1)S(1)}, bf16[256,256]{1,0:T(8,128)(2,1)S(1)}, u32[]{:S(2)}, u32[]{:S(2)}) collective-permute-start(bf16[256,256]{1,0:T(8,128)(2,1)S(1)} %get-tuple-element.46), channel_id=1, source_target_pairs={{0,4},{1,5},{2,6},{3,7},{4,0},{5,1},{6,2},{7,3},{8,12},{9,13},{10,... | collective-permute-start | bytes 393224 | tf_op jit(solution)/shard_map/ppermute | solution.py:266
  27.2 9.5 %collective-permute-start.10 = (bf16[256,256]{1,0:T(8,128)(2,1)S(1)}, bf16[256,256]{1,0:T(8,128)(2,1)S(1)}, u32[]{:S(2)}, u32[]{:S(2)}) collective-permute-start(bf16[256,256]{1,0:T(8,128)(2,1)S(1)} %get-tuple-element.42), channel_id=1, source_target_pairs={{0,2},{1,3},{2,0},{3,1},{4,6},{5,7},{6,4},{7,5},{8,10},{9,11},{10,... | collective-permute-start | bytes 393224 | tf_op jit(solution)/shard_map/ppermute | solution.py:266
  31.1 6.5 %collective-permute-start.7 = (bf16[512,128]{1,0:T(8,128)(2,1)S(1)}, bf16[512,128]{1,0:T(8,128)(2,1)S(1)}, u32[]{:S(2)}, u32[]{:S(2)}) collective-permute-start(bf16[512,128]{1,0:T(8,128)(2,1)S(1)} %get-tuple-element.38), channel_id=1, source_target_pairs={{0,2},{1,3},{2,0},{3,1},{4,6},{5,7},{6,4},{7,5},{8,10},{9,11},{10,... | collective-permute-start | bytes 393224 | tf_op jit(solution)/shard_map/ppermute | solution.py:266
  32.1 7.7 %collective-permute-start.5 = (bf16[256,128]{1,0:T(8,128)(2,1)S(1)}, bf16[256,128]{1,0:T(8,128)(2,1)S(1)}, u32[]{:S(2)}, u32[]{:S(2)}) collective-permute-start(bf16[256,128]{1,0:T(8,128)(2,1)S(1)} %get-tuple-element.36), channel_id=1, source_target_pairs={{0,4},{1,5},{2,6},{3,7},{4,0},{5,1},{6,2},{7,3},{8,12},{9,13},{10,... | collective-permute-start | bytes 196616 | tf_op jit(solution)/shard_map/ppermute | solution.py:266
  34.8 5.0 %collective-permute-start.14 = (bf16[128,256]{1,0:T(8,128)(2,1)S(1)}, bf16[128,256]{1,0:T(8,128)(2,1)S(1)}, u32[]{:S(2)}, u32[]{:S(2)}) collective-permute-start(bf16[128,256]{1,0:T(8,128)(2,1)S(1)} %get-tuple-element.48), channel_id=1, source_target_pairs={{0,1},{1,0},{2,3},{3,2},{4,5},{5,4},{6,7},{7,6},{8,9},{9,8},{10,11... | collective-permute-start | bytes 196616 | tf_op jit(solution)/shard_map/ppermute | solution.py:266
  36.7 7.5 %collective-permute-start.11 = (bf16[128,256]{1,0:T(8,128)(2,1)S(1)}, bf16[128,256]{1,0:T(8,128)(2,1)S(1)}, u32[]{:S(2)}, u32[]{:S(2)}) collective-permute-start(bf16[128,256]{1,0:T(8,128)(2,1)S(1)} %get-tuple-element.44), channel_id=1, source_target_pairs={{0,4},{1,5},{2,6},{3,7},{4,0},{5,1},{6,2},{7,3},{8,12},{9,13},{10,... | collective-permute-start | bytes 196616 | tf_op jit(solution)/shard_map/ppermute | solution.py:266
  37.7 7.3 %collective-permute-start.8 = (bf16[256,128]{1,0:T(8,128)(2,1)S(1)}, bf16[256,128]{1,0:T(8,128)(2,1)S(1)}, u32[]{:S(2)}, u32[]{:S(2)}) collective-permute-start(bf16[256,128]{1,0:T(8,128)(2,1)S(1)} %get-tuple-element.40), channel_id=1, source_target_pairs={{0,4},{1,5},{2,6},{3,7},{4,0},{5,1},{6,2},{7,3},{8,12},{9,13},{10,... | collective-permute-start | bytes 196616 | tf_op jit(solution)/shard_map/ppermute | solution.py:266
